TPU v7x, 32 devices: a whole 2x2x4 slice. The times are simulated.
32 devices in a mesh: replica: 8 (over y, x, core), fsdp: 4 (over z).
Axes of the slice: x: 2, y: 2, z: 4, core: 2. Of those that a mesh axis runs over, the one named last changes fastest.
Arguments:
- latents: bfloat16 [65536, 64], P(('replica', 'fsdp')), may hold values from -6 to 6
- target: bfloat16 [65536, 64], P(('replica', 'fsdp')), may hold values from -6 to 6
- timesteps: int32 [128], P(('replica', 'fsdp')), may hold values from 0 to 999
- patch_weight: float32 [8, 64, 5120], P('replica', None, 'fsdp'), may hold values from -0.75 to 0.75
- head_weight: float32 [8, 64, 5120], P('replica', None, 'fsdp'), may hold values from -0.078125 to 0.078125
- modulation: float32 [8, 2, 5120], P('replica', None, 'fsdp'), may hold values from -3 to 3
- time_weight: float32 [8, 256, 5120], P('replica', None, 'fsdp'), may hold values from -0.375 to 0.375
- anchor: float32 [5120, 5120], P('fsdp', 'replica'), may hold values from -6 to 6
- momentum: float32 [5120, 5120], P('fsdp', 'replica'), may hold values from -4 to 4
- frag_start: bfloat16 [5120, 5120], P('fsdp'), may hold values from -4.1 to 4.1, as said below
- frag_current: bfloat16 [8, 5120, 5120], P('replica', 'fsdp'), may hold values from -10.1 to 10.1, as said below
Outputs:
- patch_new: float32 [8, 64, 5120], P('replica', None, 'fsdp')
- head_new: float32 [8, 64, 5120], P('replica', None, 'fsdp')
- modulation_new: float32 [8, 2, 5120], P('replica', None, 'fsdp')
- time_new: float32 [8, 256, 5120], P('replica', None, 'fsdp')
- new_anchor: float32 [5120, 5120], P('fsdp', 'replica')
- new_momentum: float32 [5120, 5120], P('fsdp', 'replica')
- new_params: bfloat16 [5120, 5120], P('fsdp')
Inputs may be any that keep to these rules, and one draw needn't show every extreme that they name: `frag_start`: every entry is at least 0.02 in magnitude. `frag_current`: every entry is at least 0.02 in magnitude.
All inputs are finite; a program needn't handle non-finite values.
Results may differ from a plain program's by a relative error of at most 0.028.
Values may be sent and summed in bfloat16 or wider, within the bound.
A program may use at most 192 MiB of HBM per device.

v0:
```python
import math

import jax
import jax.numpy as jnp
from jax import lax
from jax.sharding import PartitionSpec as P

FREQ_DIM = 256
PATCH_DIM = 64
QBLOCK = 128
SAMPLE_TOKENS = 512


epsilon = 1e-06
inner_rate = 0.5
outer_rate = 0.7
momentum_decay = 0.9


def sinusoid(time_steps):
    index = jnp.arange(FREQ_DIM // 2, dtype=jnp.float32)
    frequency = jnp.exp(-math.log(10000.0) * index / (FREQ_DIM // 2))
    angles = time_steps.astype(jnp.float32)[:, None] * frequency[None, :]
    return jnp.concatenate([jnp.cos(angles), jnp.sin(angles)], axis=1)


def silu_slope(pre_act):
    sigmoid_val = jax.nn.sigmoid(pre_act)
    return sigmoid_val * (1.0 + pre_act * (1.0 - sigmoid_val))


def quantize(blocks, scale_bf):
    scale_f = scale_bf.astype(jnp.float32)[:, None, :]
    seven_abs = 7.0 * jnp.abs(blocks)
    levels = jnp.zeros_like(blocks)
    for rung_index in range(7):
        levels = levels + (seven_abs >= (rung_index + 0.5) * scale_f).astype(jnp.float32)
    return (jnp.sign(blocks) * levels).astype(jnp.bfloat16)


def make_visitor(patch_bf, head_bf, mod_bf, tok_count):

    def visit_block(totals, inputs):
        latent_blk, target_blk, embed_row = inputs
        hidden = jnp.dot(latent_blk, patch_bf, preferred_element_type=jnp.float32)
        center = hidden - jnp.mean(hidden, axis=1, keepdims=True)
        inv_std = lax.rsqrt(jnp.mean(center * center, axis=1, keepdims=True) + epsilon)
        normed = center * inv_std
        gain_row = 1.0 + mod_bf[1].astype(jnp.float32) + embed_row
        modulated = (normed * gain_row + mod_bf[0].astype(jnp.float32) + embed_row).astype(
            jnp.bfloat16
        )
        output = lax.dot_general(
            modulated, head_bf, (((1,), (1,)), ((), ())), preferred_element_type=jnp.float32
        )
        grad_out = (2.0 * (output - target_blk.astype(jnp.float32)) / tok_count).astype(
            jnp.bfloat16
        )
        grad_head = lax.dot_general(
            grad_out, modulated, (((0,), (0,)), ((), ())), preferred_element_type=jnp.float32
        )
        grad_mixed = jnp.dot(grad_out, head_bf, preferred_element_type=jnp.float32)
        grad_shift = jnp.sum(grad_mixed, axis=0)
        grad_scale = jnp.sum(grad_mixed * normed, axis=0)
        grad_normed = grad_mixed * gain_row
        grad_hidden = (
            (
                grad_normed
                - jnp.mean(grad_normed, axis=1, keepdims=True)
                - normed * jnp.mean(grad_normed * normed, axis=1, keepdims=True)
            )
            * inv_std
        ).astype(jnp.bfloat16)
        grad_patch = lax.dot_general(
            latent_blk, grad_hidden, (((0,), (0,)), ((), ())), preferred_element_type=jnp.float32
        )
        new_totals = (
            totals[0] + grad_patch,
            totals[1] + grad_head,
            totals[2] + jnp.stack([grad_shift, grad_scale]),
        )
        return (new_totals, grad_shift + grad_scale)

    return visit_block


def per_device(
    latents,
    target,
    timesteps,
    patch_weight,
    head_weight,
    modulation,
    time_weight,
    anchor,
    momentum,
    frag_start,
    frag_current,
):
    fsdp_count = lax.axis_size("fsdp")
    replica_count = lax.axis_size("replica")
    delta = frag_start.astype(jnp.float32) - frag_current[0].astype(jnp.float32)
    row_count = delta.shape[0]
    block_count = row_count // QBLOCK
    blocks = delta.reshape(block_count, QBLOCK, delta.shape[1])
    scale = (jnp.max(jnp.abs(blocks), axis=1) + epsilon).astype(jnp.bfloat16)
    code = quantize(blocks, scale)
    terms = (code.astype(jnp.float32) * scale.astype(jnp.float32)[:, None, :] / 7.0).reshape(
        delta.shape
    )
    total = lax.psum_scatter(
        terms.astype(jnp.bfloat16), "replica", scatter_dimension=1, tiled=True
    ).astype(jnp.float32)
    average = total / replica_count
    new_momentum = momentum_decay * momentum + average
    new_anchor = anchor - outer_rate * (average + momentum_decay * new_momentum)
    new_params = lax.all_gather(new_anchor.astype(jnp.bfloat16), "replica", axis=1, tiled=True)
    samples_here = timesteps.shape[0]
    tok_count = latents.shape[0] * fsdp_count * 1.0
    sines = sinusoid(timesteps).astype(jnp.bfloat16)
    sines_cols = sines.T
    patch_local = patch_weight[0].astype(jnp.bfloat16)
    head_local = head_weight[0].astype(jnp.bfloat16)
    mod_local = modulation[0].astype(jnp.bfloat16)
    time_local = time_weight[0].astype(jnp.bfloat16)
    patch_bf, head_bf, mod_bf, time_bf = (
        lax.all_gather(patch_local, "fsdp", axis=1, tiled=True),
        lax.all_gather(head_local, "fsdp", axis=1, tiled=True),
        lax.all_gather(mod_local, "fsdp", axis=1, tiled=True),
        lax.all_gather(time_local, "fsdp", axis=1, tiled=True),
    )
    pre_act = jnp.dot(sines, time_bf, preferred_element_type=jnp.float32)
    embed = jax.nn.silu(pre_act)
    width = patch_bf.shape[1]
    latent_blocks = latents.reshape(samples_here, SAMPLE_TOKENS, PATCH_DIM)
    target_blocks = target.reshape(samples_here, SAMPLE_TOKENS, PATCH_DIM)
    start_totals = (
        jnp.zeros((PATCH_DIM, width), jnp.float32),
        jnp.zeros((PATCH_DIM, width), jnp.float32),
        jnp.zeros((2, width), jnp.float32),
    )
    totals, grad_embed = lax.scan(
        make_visitor(patch_bf, head_bf, mod_bf, tok_count),
        start_totals,
        (latent_blocks, target_blocks, embed),
    )
    grad_pre = (grad_embed * silu_slope(pre_act)).astype(jnp.bfloat16)
    grad_time_full = jnp.dot(sines_cols, grad_pre, preferred_element_type=jnp.float32)
    grad_patch, grad_head, grad_mod, grad_time = (
        lax.psum_scatter(
            totals[0].astype(jnp.bfloat16), "fsdp", scatter_dimension=1, tiled=True
        ).astype(jnp.float32),
        lax.psum_scatter(
            totals[1].astype(jnp.bfloat16), "fsdp", scatter_dimension=1, tiled=True
        ).astype(jnp.float32),
        lax.psum_scatter(
            totals[2].astype(jnp.bfloat16), "fsdp", scatter_dimension=1, tiled=True
        ).astype(jnp.float32),
        lax.psum_scatter(
            grad_time_full.astype(jnp.bfloat16), "fsdp", scatter_dimension=1, tiled=True
        ).astype(jnp.float32),
    )
    patch_new = patch_weight - inner_rate * grad_patch[None]
    head_new = head_weight - inner_rate * grad_head[None]
    modulation_new = modulation - inner_rate * grad_mod[None]
    time_new = time_weight - inner_rate * grad_time[None]
    return (patch_new, head_new, modulation_new, time_new, new_anchor, new_momentum, new_params)


def solution(mesh):
    in_specs = (
        P(("replica", "fsdp"), None),
        P(("replica", "fsdp"), None),
        P(("replica", "fsdp")),
        P("replica", None, "fsdp"),
        P("replica", None, "fsdp"),
        P("replica", None, "fsdp"),
        P("replica", None, "fsdp"),
        P("fsdp", "replica"),
        P("fsdp", "replica"),
        P("fsdp", None),
        P("replica", "fsdp", None),
    )
    out_specs = (
        P("replica", None, "fsdp"),
        P("replica", None, "fsdp"),
        P("replica", None, "fsdp"),
        P("replica", None, "fsdp"),
        P("fsdp", "replica"),
        P("fsdp", "replica"),
        P("fsdp", None),
    )
    return jax.shard_map(
        per_device, mesh=mesh, in_specs=in_specs, out_specs=out_specs, check_vma=False
    )
```

profile of v0, /device:TPU:0, one launch (start us, length us, event | category | flops | bytes accessed | tf_op | source)
XLA Modules:
  0.0 479.8 jit_solution(12674832139696244603)
XLA Ops:
  8.0 2.2 convert_element_type.210
  10.3 19.1 %fusion.11 = f32[1280,5120]{1,0:T(8,128)} fusion(bf16[1280,5120]{1,0:T(8,128)(2,1)} %param.22, bf16[1,1280,5120]{2,1,0:T(8,128)(2,1)} %param.23), kind=kLoop, calls=%fused_computation.39 | loop fusion | flops 26214400 | bytes 52428800 | tf_op jit(solution)/shard_map/abs | solution.py:34
  29.5 10.2 %reduce_max.9 = f32[10,5120]{1,0:T(8,128)S(1)} reduce(f32[10,128,5120]{2,1,0:T(8,128)} %bitcast.134, f32[]{:T(128)} %constant.92.clone.1), dimensions={1}, to_apply=%region_12.13 | reduce | flops 6502400 | bytes 26419204 | tf_op jit(solution)/shard_map/reduce_max | solution.py:106
  40.0 33.4 %fusion.10 = bf16[1280,5120]{1,0:T(8,128)(2,1)} fusion(f32[10,5120]{1,0:T(8,128)S(1)} %convert_element_type.227, f32[10,5120]{1,0:T(8,128)S(1)} %get-tuple-element.252, f32[10,5120]{1,0:T(8,128)S(1)} %get-tuple-element.251, f32[10,5120]{1,0:T(8,128)S(1)} %get-tuple-element.250, f32[10,5120]{1,0:T(8,128)S(1)} %get-tuple-element.249, ...), kind=kLoop, calls=%fused_computation.30 | loop fusion | flops 209715200 | bytes 40960000 | tf_op jit(solution)/shard_map/convert_element_type | solution.py:112
  73.4 17.7 %copy.25 = bf16[1280,5120]{0,1:T(8,128)(2,1)} copy(bf16[1280,5120]{1,0:T(8,128)(2,1)} %fusion.10) | data formatting | bytes 26214400
  91.8 14.8 %all-gather.1 = bf16[1,2,5120]{2,1,0:T(2,128)(2,1)S(1)} all-gather(bf16[1,2,1280]{2,1,0:T(2,128)(2,1)S(1)} %convert_element_type.207), channel_id=3, replica_groups=mesh['replica'=8,'fsdp'=4] {'fsdp'}, dimensions={2}, use_global_device_ids=true | all-gather | bytes 25600 | tf_op jit(solution)/shard_map/all_gather | solution.py:129
  107.4 17.4 %all-gather.3 = bf16[1,64,5120]{2,1,0:T(8,128)(2,1)} all-gather(bf16[1,64,1280]{2,1,0:T(8,128)(2,1)S(1)} %convert_element_type.212), channel_id=5, replica_groups=mesh['replica'=8,'fsdp'=4] {'fsdp'}, dimensions={2}, use_global_device_ids=true | all-gather | bytes 819200 | tf_op jit(solution)/shard_map/all_gather | solution.py:128
  124.8 16.6 %all-gather = bf16[1,64,5120]{2,1,0:T(8,128)(2,1)S(1)} all-gather(bf16[1,64,1280]{2,1,0:T(8,128)(2,1)S(1)} %convert_element_type.205), channel_id=2, replica_groups=mesh['replica'=8,'fsdp'=4] {'fsdp'}, dimensions={2}, use_global_device_ids=true | all-gather | bytes 819200 | tf_op jit(solution)/shard_map/all_gather | solution.py:127
  141.4 1.2 copy.21
  142.8 2.9 fusion.15
  145.6 106.1 %while.19 = (s32[]{:T(128)}, f32[64,5120]{1,0:T(8,128)}, f32[64,5120]{1,0:T(8,128)S(1)}, f32[2,5120]{1,0:T(2,128)}, f32[4,5120]{1,0:T(4,128)}, /*index=5*/bf16[4...) while((s32[]{:T(128)}, f32[64,5120]{1,0:T(8,128)}, ...), condition=%wide.region_7.8_spmd.clone, body=%wide.region_0.7_spmd.clone.sunk | while | flops 1749988864 | bytes 110811440 | solution.py:142
  145.6 0.9 add_add_fusion.2
  146.6 1.6 fusion.48
  148.2 1.2 multiply_reduce_fusion.6
  149.4 5.0 %add_convert_fusion.4 = bf16[512,5120]{1,0:T(8,128)(2,1)} fusion(f32[512,5120]{1,0:T(8,128)S(1)} %get-tuple-element.335, f32[5120]{0:T(1024)S(1)} %bitcast.144, f32[5120]{0:T(1024)S(1)} %bitcast.145, f32[5120]{0:T(1024)S(1)} %bitcast.140, f32[512]{0:T(512)S(1)} %add_rsqrt_fusion.2, f32[512]{0:T(512)S(1)} %broadcast_multiply_fusion.5), kind=kLoop, calls=%fused_computation.3.clone.1 | loop fusion | flops 15728640 | bytes 15794176 | tf_op jit(solution)/shard_map/while/body/eval_jaxpr/convert_element_type | solution.py:50
  154.3 4.5 fusion.49
  158.8 3.7 convolution_add_fusion.5
  162.5 3.7 multiply_reduce_fusion.7
  166.2 3.1 convolution_add_fusion.4
  169.3 1.0 copy-done.1
  170.5 1.6 dynamic_update_slice.9
  173.1 1.6 fusion.48
  174.7 1.2 multiply_reduce_fusion.6
  175.9 5.0 %add_convert_fusion.4 = bf16[512,5120]{1,0:T(8,128)(2,1)} fusion(f32[512,5120]{1,0:T(8,128)S(1)} %get-tuple-element.335, f32[5120]{0:T(1024)S(1)} %bitcast.144, f32[5120]{0:T(1024)S(1)} %bitcast.145, f32[5120]{0:T(1024)S(1)} %bitcast.140, f32[512]{0:T(512)S(1)} %add_rsqrt_fusion.2, f32[512]{0:T(512)S(1)} %broadcast_multiply_fusion.5), kind=kLoop, calls=%fused_computation.3.clone.1 | loop fusion | flops 15728640 | bytes 15794176 | tf_op jit(solution)/shard_map/while/body/eval_jaxpr/convert_element_type | solution.py:50
  180.8 4.5 fusion.49
  185.3 3.7 convolution_add_fusion.5
  189.0 3.7 multiply_reduce_fusion.7
  192.7 3.1 convolution_add_fusion.4
  195.9 1.0 copy-done.1
  197.0 1.6 dynamic_update_slice.9
  199.6 1.6 fusion.48
  201.2 1.2 multiply_reduce_fusion.6
  202.4 5.0 %add_convert_fusion.4 = bf16[512,5120]{1,0:T(8,128)(2,1)} fusion(f32[512,5120]{1,0:T(8,128)S(1)} %get-tuple-element.335, f32[5120]{0:T(1024)S(1)} %bitcast.144, f32[5120]{0:T(1024)S(1)} %bitcast.145, f32[5120]{0:T(1024)S(1)} %bitcast.140, f32[512]{0:T(512)S(1)} %add_rsqrt_fusion.2, f32[512]{0:T(512)S(1)} %broadcast_multiply_fusion.5), kind=kLoop, calls=%fused_computation.3.clone.1 | loop fusion | flops 15728640 | bytes 15794176 | tf_op jit(solution)/shard_map/while/body/eval_jaxpr/convert_element_type | solution.py:50
  207.4 4.5 fusion.49
  211.8 3.7 convolution_add_fusion.5
  215.5 3.7 multiply_reduce_fusion.7
  219.2 3.1 convolution_add_fusion.4
  222.4 1.0 copy-done.1
  223.5 1.6 dynamic_update_slice.9
  225.2 0.9 add_add_fusion.2
  226.1 1.6 fusion.48
  227.7 1.2 multiply_reduce_fusion.6
  228.9 5.0 %add_convert_fusion.4 = bf16[512,5120]{1,0:T(8,128)(2,1)} fusion(f32[512,5120]{1,0:T(8,128)S(1)} %get-tuple-element.335, f32[5120]{0:T(1024)S(1)} %bitcast.144, f32[5120]{0:T(1024)S(1)} %bitcast.145, f32[5120]{0:T(1024)S(1)} %bitcast.140, f32[512]{0:T(512)S(1)} %add_rsqrt_fusion.2, f32[512]{0:T(512)S(1)} %broadcast_multiply_fusion.5), kind=kLoop, calls=%fused_computation.3.clone.1 | loop fusion | flops 15728640 | bytes 15794176 | tf_op jit(solution)/shard_map/while/body/eval_jaxpr/convert_element_type | solution.py:50
  233.9 4.5 fusion.49
  238.3 3.7 convolution_add_fusion.5
  242.0 3.7 multiply_reduce_fusion.7
  245.8 3.1 convolution_add_fusion.4
  248.9 1.0 copy-done.1
  250.1 1.6 dynamic_update_slice.9
  252.5 1.6 copy.23
  254.2 2.2 convert_element_type.214
  257.5 3.3 convolution_convert_fusion
  260.9 2.9 copy.26
  263.8 7.3 %fusion.21 = (bf16[1280,640]{1,0:T(8,128)(2,1)}, f32[1280,640]{1,0:T(8,128)}, f32[1280,640]{1,0:T(8,128)}) fusion(f32[1280,640]{1,0:T(8,128)} %param.20, bf16[1280,640]{1,0:T(8,128)(2,1)S(1)} %copy.26, f32[1280,640]{1,0:T(8,128)} %param.21), kind=kLoop, calls=%fused_computation.72 | loop fusion | flops 7372800 | bytes 16384000 | tf_op jit(solution)/shard_map/convert_element_type | solution.py:117
  271.2 13.8 %reduce-scatter.16.cloned.1.call-done = bf16[1280,2]{1,0:T(8,128)(2,1)} async-done(((bf16[5120,2]{1,0:T(8,128)(2,1)}), bf16[1280,2]{1,0:T(8,128)(2,1)}) %reduce-scatter.16.cloned.1.call-update) | async-done | bytes 5136
  285.0 1.1 copy.24
  286.8 21.5 %reduce-scatter.10.cloned.1.call-done = bf16[64,1280]{1,0:T(8,128)(2,1)} async-done(((bf16[64,5120]{1,0:T(8,128)(2,1)}), bf16[64,1280]{1,0:T(8,128)(2,1)}) %reduce-scatter.10.cloned.1.call-update) | async-done | bytes 163856 | tf_op jit(solution)/shard_map/reduce_scatter | solution.py:150
  308.3 1.7 bitcast_subtract_fusion.2
  310.0 22.3 %reduce-scatter.12.cloned.1.call-done = bf16[64,1280]{1,0:T(8,128)(2,1)} async-done(((bf16[64,5120]{1,0:T(8,128)(2,1)}), bf16[64,1280]{1,0:T(8,128)(2,1)}) %reduce-scatter.12.cloned.1.call-update) | async-done | bytes 163856 | tf_op jit(solution)/shard_map/reduce_scatter | solution.py:153
  332.3 1.8 bitcast_subtract_fusion.1
  334.0 52.0 %reduce-scatter.14.cloned.1.call-done = bf16[256,1280]{1,0:T(8,128)(2,1)} async-done(((bf16[256,5120]{1,0:T(8,128)(2,1)}), bf16[256,1280]{1,0:T(8,128)(2,1)}) %reduce-scatter.14.cloned.1.call-update) | async-done | bytes 655376 | tf_op jit(solution)/shard_map/reduce_scatter | solution.py:159
  386.0 2.3 bitcast_subtract_fusion
  388.3 73.2 %all-gather.7.cloned.1.call-done = bf16[1280,5120]{1,0:T(8,128)(2,1)} async-done(((bf16[1280,640]{1,0:T(8,128)(2,1)}), bf16[1280,5120]{1,0:T(8,128)(2,1)}) %all-gather.7.cloned.1.call-update) | async-done | bytes 13107216 | tf_op jit(solution)/shard_map/all_gather | solution.py:117
  461.6 10.8 %copy.47 = bf16[1280,5120]{1,0:T(8,128)(2,1)} copy(bf16[1280,5120]{1,0:T(8,128)(2,1)} %all-gather.7.cloned.1.call-done) | data formatting | bytes 26214400
  (111 shorter events, 7.0 us)
Async XLA Ops:
  8.0 134.8 %all-gather.9.cloned.1.call-start = ((), (), s32[]{:S(2)}) async-start(), calls=%async_computation.9 | async-start | bytes 3276800 | tf_op jit(solution)/shard_map/all_gather | solution.py:130
  10.3 250.6 %reduce-scatter.18.cloned.1.call-start = ((), (), s32[]{:S(2)}) async-start(), calls=%async_computation.11 | async-start | bytes 14745600
  91.0 0.7 copy-start.12
  91.0 0.7 copy-start.10
  91.0 15.5 %copy-start.6 = (f32[1,64,1280]{2,1,0:T(8,128)S(1)}, f32[1,64,1280]{2,1,0:T(8,128)}, u32[]{:S(2)}) copy-start(f32[1,64,1280]{2,1,0:T(8,128)} %param.16) | copy-start | bytes 983044
  91.0 15.5 %copy-start.8 = (f32[1,64,1280]{2,1,0:T(8,128)S(1)}, f32[1,64,1280]{2,1,0:T(8,128)}, u32[]{:S(2)}) copy-start(f32[1,64,1280]{2,1,0:T(8,128)} %param.17) | copy-start | bytes 983044
  91.1 15.6 %copy-start.9 = (bf16[2048,64]{0,1:T(8,128)(2,1)S(1)}, bf16[2048,64]{0,1:T(8,128)(2,1)}, u32[]{:S(2)}) copy-start(bf16[2048,64]{0,1:T(8,128)(2,1)} %param.14) | copy-start | bytes 786436
  91.1 193.9 %reduce-scatter.16.cloned.1.call-start = ((), (), s32[]{:S(2)}) async-start(), calls=%async_computation.10 | async-start | bytes 1638400
  154.3 8.1 %copy-start.2 = (bf16[64,5120]{1,0:T(8,128)(2,1)S(1)}, bf16[64,5120]{1,0:T(8,128)(2,1)}, u32[]{:S(2)}) copy-start(bf16[64,5120]{1,0:T(8,128)(2,1)} %get-tuple-element.381) | copy-start | bytes 1966084 | tf_op jit(solution)/shard_map/while
  162.5 3.7 copy-start
  166.2 4.2 copy-start.4
  169.3 1.1 copy-start.1
  170.5 1.6 copy-start.5
  180.8 8.1 %copy-start.2 = (bf16[64,5120]{1,0:T(8,128)(2,1)S(1)}, bf16[64,5120]{1,0:T(8,128)(2,1)}, u32[]{:S(2)}) copy-start(bf16[64,5120]{1,0:T(8,128)(2,1)} %get-tuple-element.381) | copy-start | bytes 1966084 | tf_op jit(solution)/shard_map/while
  189.0 3.7 copy-start
  192.7 4.2 copy-start.4
  195.8 1.1 copy-start.1
  197.0 1.6 copy-start.5
  207.4 8.1 %copy-start.2 = (bf16[64,5120]{1,0:T(8,128)(2,1)S(1)}, bf16[64,5120]{1,0:T(8,128)(2,1)}, u32[]{:S(2)}) copy-start(bf16[64,5120]{1,0:T(8,128)(2,1)} %get-tuple-element.381) | copy-start | bytes 1966084 | tf_op jit(solution)/shard_map/while
  215.5 3.7 copy-start
  219.2 4.2 copy-start.4
  222.4 1.1 copy-start.1
  223.5 1.6 copy-start.5
  233.9 8.1 %copy-start.2 = (bf16[64,5120]{1,0:T(8,128)(2,1)S(1)}, bf16[64,5120]{1,0:T(8,128)(2,1)}, u32[]{:S(2)}) copy-start(bf16[64,5120]{1,0:T(8,128)(2,1)} %get-tuple-element.381) | copy-start | bytes 1966084 | tf_op jit(solution)/shard_map/while
  242.0 3.7 copy-start
  245.8 4.2 copy-start.4
  248.9 1.1 copy-start.1
  250.0 1.6 copy-start.5
  254.1 54.2 %reduce-scatter.10.cloned.1.call-start = ((), (), s32[]{:S(2)}) async-start(), calls=%async_computation.5 | async-start | bytes 819200 | tf_op jit(solution)/shard_map/reduce_scatter | solution.py:150
  256.4 75.8 %reduce-scatter.12.cloned.1.call-start = ((), (), s32[]{:S(2)}) async-start(), calls=%async_computation.6 | async-start | bytes 819200 | tf_op jit(solution)/shard_map/reduce_scatter | solution.py:153
  257.4 128.6 %reduce-scatter.14.cloned.1.call-start = ((), (), s32[]{:S(2)}) async-start(), calls=%async_computation.7 | async-start | bytes 3276800 | tf_op jit(solution)/shard_map/reduce_scatter | solution.py:159
  260.8 200.8 %all-gather.7.cloned.1.call-start = ((), (), s32[]{:S(2)}) async-start(), calls=%async_computation.8 | async-start | bytes 14745600 | tf_op jit(solution)/shard_map/all_gather | solution.py:117
  260.9 25.3 %copy-start.11 = (f32[1,2,1280]{2,1,0:T(2,128)S(1)}, f32[1,2,1280]{2,1,0:T(2,128)}, u32[]{:S(2)}) copy-start(f32[1,2,1280]{2,1,0:T(2,128)} %param.18) | copy-start | bytes 30724
  260.9 47.4 %copy-start.7 = (f32[1,64,1280]{2,1,0:T(8,128)S(1)}, f32[1,64,1280]{2,1,0:T(8,128)}, u32[]{:S(2)}) copy-start(f32[1,64,1280]{2,1,0:T(8,128)} %param.16) | copy-start | bytes 983044
  263.8 122.2 %copy-start.3 = (f32[1,256,1280]{2,1,0:T(8,128)S(1)}, f32[1,256,1280]{2,1,0:T(8,128)}, u32[]{:S(2)}) copy-start(f32[1,256,1280]{2,1,0:T(8,128)} %param.19) | copy-start | bytes 3932164
Sparse Core Ops, SparseCore 0:
  11.0 57.4 all-gather.8
Sparse Core Ops, SparseCore 1:
  91.2 97.6 reduce-scatter.17
  254.2 30.8 reduce-scatter.15
  287.2 21.0 reduce-scatter.9
  311.2 21.0 reduce-scatter.11
  335.2 50.8 reduce-scatter.13
  388.0 73.5 all-gather.6
where the time goes:
time: 481 us; the launch traced here: 480 us
  waiting for transfers between devices  183 us (38%)
  other arithmetic  112 us (23%)
  matrix products  72.3 us (15%)
  blocking collectives  48.8 us (10%)
  local copies, waits for them, and re-layouts  47.4 us (10%)
  between operations  15.7 us (3%)
    all_gather x1, waiting for transfers between devices, per_device(): lax.all_gather(new_anchor.astype(jnp.bfloat16), 'replica', axis=1, tiled=...  73.2 us
    reduce_scatter x1, waiting for transfers between devices, per_device(): lax.psum_scatter(grad_time_full.astype(jnp.bfloat16), 'fsdp', scatter_dim...  52 us
    unnamed x22, local copies, waits for them, and re-layouts  35.9 us
    convert_element_type x1, other arithmetic, per_device(): terms.astype(jnp.bfloat16)  33.4 us
    reduce_scatter x1, waiting for transfers between devices, per_device(): lax.psum_scatter(totals[1].astype(jnp.bfloat16), 'fsdp', scatter_dimensio...  22.3 us
    reduce_scatter x1, waiting for transfers between devices, per_device(): lax.psum_scatter(totals[0].astype(jnp.bfloat16), 'fsdp', scatter_dimensio...  21.5 us
    convert_element_type x4, other arithmetic, visit_block(): (normed * gain_row + mod_bf[0].astype(jnp.float32) + embed_row).astype(jn...  19.8 us
    abs x1, other arithmetic, quantize(): seven_abs = 7.0 * jnp.abs(blocks)  19.1 us
  transfers between devices with their start and end apart: 7, of which 5 were waited for; matrix products, arithmetic and copies ran while one was open for 45% of the time, Pallas kernels for 0%

commit v1 on v0

v1 whole, which is shorter than its diff:
```python
import math

import jax
import jax.numpy as jnp
from jax import lax
from jax.experimental import pallas as pl
from jax.experimental.pallas import tpu as pltpu
from jax.sharding import PartitionSpec as P

FREQ_DIM = 256
PATCH_DIM = 64
QBLOCK = 128
SAMPLE_TOKENS = 512

epsilon = 1e-06
inner_rate = 0.5
outer_rate = 0.7
momentum_decay = 0.9

MESH = pl.DeviceIdType.MESH
EXACT = lax.Precision.HIGHEST
TIE_UP = 1.0 + 2.0**-22


def sinusoid(time_steps):
    index = jnp.arange(FREQ_DIM // 2, dtype=jnp.float32)
    frequency = jnp.exp(-math.log(10000.0) * index / (FREQ_DIM // 2))
    angles = time_steps.astype(jnp.float32)[:, None] * frequency[None, :]
    return jnp.concatenate([jnp.cos(angles), jnp.sin(angles)], axis=1)


def silu_slope(pre_act):
    sigmoid_val = jax.nn.sigmoid(pre_act)
    return sigmoid_val * (1.0 + pre_act * (1.0 - sigmoid_val))


def fdot(spec, a, b):
    return jnp.einsum(spec, a, b, precision=EXACT, preferred_element_type=jnp.float32)


def nearest(values):
    return lax.round(values, lax.RoundingMethod.TO_NEAREST_EVEN)


def flip(index, bit):
    return index + bit - 2 * bit * lax.rem(index // bit, 2)


def fragment_kernel(
    blocks,
    cols,
    start_hbm,
    cur_hbm,
    anchor_hbm,
    mom_hbm,
    anchor_out,
    mom_out,
    params_out,
    start_v,
    cur_v,
    terms,
    got1,
    got2,
    got3,
    anchor_v,
    mom_v,
    own,
    load_sem,
    state_sem,
    store_sem,
    s_send,
    s_recv,
    g_send,
    g_recv,
    own_sem,
):
    me = lax.axis_index("replica")
    core = lax.rem(me, 2)
    rows = QBLOCK
    sibling = flip(me, 1)

    def load(i, slot):
        span = pl.ds(pl.multiple_of(i * rows, rows), rows)
        return (
            pltpu.make_async_copy(start_hbm.at[span, :], start_v.at[slot], load_sem.at[slot, 0]),
            pltpu.make_async_copy(cur_hbm.at[span, :], cur_v.at[slot], load_sem.at[slot, 1]),
        )

    def bits(i):
        first = 2 + 2 * lax.rem(i, 2)
        return first, 6 - first

    def send(src, dst, send_sem, recv_sem, to):
        return pltpu.make_async_remote_copy(
            src_ref=src,
            dst_ref=dst,
            send_sem=send_sem,
            recv_sem=recv_sem,
            device_id={"replica": to},
            device_id_type=MESH,
        )

    def pair_at(who, fixed, other, k):
        chip = who // 2
        f, o = fixed // 2, other // 2
        return f * lax.rem(chip // f, 2) + o * k

    def step1(i):
        return send(
            terms.at[i, 1 - core], got1.at[i], s_send.at[0, i], s_recv.at[0, i], sibling
        )

    def step2(i):
        first, second = bits(i)
        to = flip(me, first)
        return [
            send(
                terms.at[i, core, pair_at(to, first, second, k)],
                got2.at[i, k],
                s_send.at[1 + k, i],
                s_recv.at[1 + k, i],
                to,
            )
            for k in range(2)
        ]

    def step3(i):
        first, second = bits(i)
        to = flip(me, second)
        return send(
            terms.at[i, core, to // 2], got3.at[i], s_send.at[3, i], s_recv.at[3, i], to
        )

    def place(i, who):
        span = pl.ds(pl.multiple_of(i * rows, rows), rows)
        return params_out.at[span, pl.ds(pl.multiple_of(who * cols, 128), cols)]

    def back3(i):
        first, second = bits(i)
        return send(
            own.at[i], place(i, me), g_send.at[0, i], g_recv.at[0, i], flip(me, second)
        )

    def back2(i):
        first, second = bits(i)
        to = flip(me, first)
        near = flip(me, second)
        return [
            send(own.at[i], place(i, me), g_send.at[1, i], g_recv.at[1, i], to),
            send(place(i, near), place(i, near), g_send.at[2, i], g_recv.at[2, i], to),
        ]

    def back1(i):
        first, second = bits(i)
        whos = (flip(me, second), flip(me, first), flip(flip(me, first), second))
        sends = [send(own.at[i], place(i, me), g_send.at[3, i], g_recv.at[3, i], sibling)]
        for n, who in enumerate(whos):
            sends.append(
                send(place(i, who), place(i, who), g_send.at[4 + n, i], g_recv.at[4 + n, i], sibling)
            )
        return sends

    def keep(i):
        return pltpu.make_async_copy(own.at[i], place(i, me), own_sem.at[i])

    state_loads = (
        pltpu.make_async_copy(anchor_hbm, anchor_v, state_sem.at[0]),
        pltpu.make_async_copy(mom_hbm, mom_v, state_sem.at[1]),
    )
    for copy in load(0, 0):
        copy.start()
    for copy in state_loads:
        copy.start()

    barrier = pltpu.get_barrier_semaphore()
    for bit in (1, 2, 4):
        pl.semaphore_signal(
            barrier, inc=1, device_id={"replica": flip(me, bit)}, device_id_type=MESH
        )
    pl.semaphore_wait(barrier, 3)

    def quantize(i):
        slot = lax.rem(i, 2)
        for copy in load(i, slot):
            copy.wait()

        @pl.when(i + 1 < blocks)
        def _():
            for copy in load(i + 1, 1 - slot):
                copy.start()

        for who in range(8):
            for part in range(cols // 128):
                lanes = pl.ds(who * cols + part * 128, 128)
                delta = start_v[slot, :, lanes].astype(jnp.float32) - cur_v[
                    slot, :, lanes
                ].astype(jnp.float32)
                top = jnp.max(jnp.abs(delta), axis=0, keepdims=True)
                scale = (top + epsilon).astype(jnp.bfloat16).astype(jnp.float32)
                level = nearest(delta * (7.0 * TIE_UP / scale))
                level = jnp.clip(level, -7.0, 7.0)
                terms[i, who % 2, who // 2, :, pl.ds(part * 128, 128)] = (
                    level * (scale / 7.0)
                ).astype(jnp.bfloat16)
        step1(i).start()

    def fold1(i):
        step1(i).wait()
        for k in range(4):
            terms[i, core, k] = (
                terms[i, core, k].astype(jnp.float32) + got1[i, k].astype(jnp.float32)
            ).astype(jnp.bfloat16)
        for copy in step2(i):
            copy.start()

    def fold2(i):
        for copy in step2(i):
            copy.wait()
        first, second = bits(i)
        for k in range(2):
            at = pair_at(me, first, second, k)
            terms[i, core, at] = (
                terms[i, core, at].astype(jnp.float32) + got2[i, k].astype(jnp.float32)
            ).astype(jnp.bfloat16)
        step3(i).start()

    def update(i):
        step3(i).wait()

        @pl.when(i == 0)
        def _():
            for copy in state_loads:
                copy.wait()

        span = pl.ds(pl.multiple_of(i * rows, rows), rows)
        average = (
            terms[i, core, me // 2].astype(jnp.float32) + got3[i].astype(jnp.float32)
        ) / 8.0
        new_momentum = momentum_decay * mom_v[span, :] + average
        new_anchor = anchor_v[span, :] - outer_rate * (average + momentum_decay * new_momentum)
        mom_v[span, :] = new_momentum
        anchor_v[span, :] = new_anchor
        own[i] = new_anchor.astype(jnp.bfloat16)
        back3(i).start()
        keep(i).start()
        pltpu.make_async_copy(anchor_v.at[span, :], anchor_out.at[span, :], store_sem.at[0, i]).start()
        pltpu.make_async_copy(mom_v.at[span, :], mom_out.at[span, :], store_sem.at[1, i]).start()

    def spread2(i):
        back3(i).wait()
        for copy in back2(i):
            copy.start()

    def spread1(i):
        for copy in back2(i):
            copy.wait()
        for copy in back1(i):
            copy.start()

    stages = ((0, quantize), (1, fold1), (3, fold2), (5, update), (7, spread2), (9, spread1))

    def step(i, carry):
        for lag, stage in stages:

            @pl.when(jnp.logical_and(i >= lag, i < blocks + lag))
            def _(stage=stage, lag=lag):
                stage(i - lag)

        return carry

    lax.fori_loop(0, blocks + stages[-1][0], step, 0)

    def finish(i, carry):
        span = pl.ds(pl.multiple_of(i * rows, rows), rows)
        for copy in back1(i):
            copy.wait()
        keep(i).wait()
        pltpu.make_async_copy(anchor_v.at[span, :], anchor_out.at[span, :], store_sem.at[0, i]).wait()
        pltpu.make_async_copy(mom_v.at[span, :], mom_out.at[span, :], store_sem.at[1, i]).wait()
        return carry

    lax.fori_loop(0, blocks, finish, 0)


def fragment_by_kernel(anchor, momentum, frag_start, frag_current):
    rows, width = frag_start.shape
    blocks, cols = rows // QBLOCK, anchor.shape[1]
    bf16, f32 = jnp.bfloat16, jnp.float32
    dma = pltpu.SemaphoreType.DMA
    return pl.pallas_call(
        lambda *refs: fragment_kernel(blocks, cols, *refs),
        out_shape=(
            jax.ShapeDtypeStruct((rows, cols), f32),
            jax.ShapeDtypeStruct((rows, cols), f32),
            jax.ShapeDtypeStruct((rows, width), bf16),
        ),
        in_specs=[pl.BlockSpec(memory_space=pl.ANY)] * 4,
        out_specs=(pl.BlockSpec(memory_space=pl.ANY),) * 3,
        scratch_shapes=[
            pltpu.VMEM((2, QBLOCK, width), bf16),
            pltpu.VMEM((2, QBLOCK, width), bf16),
            pltpu.VMEM((blocks, 2, 4, QBLOCK, cols), bf16),
            pltpu.VMEM((blocks, 4, QBLOCK, cols), bf16),
            pltpu.VMEM((blocks, 2, QBLOCK, cols), bf16),
            pltpu.VMEM((blocks, QBLOCK, cols), bf16),
            pltpu.VMEM((rows, cols), f32),
            pltpu.VMEM((rows, cols), f32),
            pltpu.VMEM((blocks, QBLOCK, cols), bf16),
            dma((2, 2)),
            dma((2,)),
            dma((2, blocks)),
            dma((4, blocks)),
            dma((4, blocks)),
            dma((7, blocks)),
            dma((7, blocks)),
            dma((blocks,)),
        ],
        compiler_params=pltpu.CompilerParams(
            collective_id=0, has_side_effects=True, vmem_limit_bytes=56 * 1024 * 1024
        ),
        cost_estimate=pl.CostEstimate(
            flops=20 * rows * width, bytes_accessed=8 * rows * width, transcendentals=0
        ),
        name="fragment_sync",
    )(frag_start, frag_current, anchor, momentum)


def fragment_by_collectives(anchor, momentum, frag_start, frag_current):
    replica_count = lax.axis_size("replica")
    delta = frag_start.astype(jnp.float32) - frag_current.astype(jnp.float32)
    rows, width = delta.shape
    blocks = delta.reshape(rows // QBLOCK, QBLOCK, width)
    top = jnp.max(jnp.abs(blocks), axis=1, keepdims=True)
    scale = lax.reduce_precision(top + epsilon, 8, 7)
    level = jnp.clip(nearest(blocks * (7.0 * TIE_UP / scale)), -7.0, 7.0)
    terms = (level * (scale / 7.0)).astype(jnp.bfloat16).reshape(rows, width)
    total = lax.psum_scatter(terms, "replica", scatter_dimension=1, tiled=True)
    average = total.astype(jnp.float32) / replica_count
    new_momentum = momentum_decay * momentum + average
    new_anchor = anchor - outer_rate * (average + momentum_decay * new_momentum)
    new_params = lax.all_gather(new_anchor.astype(jnp.bfloat16), "replica", axis=1, tiled=True)
    return new_anchor, new_momentum, new_params


def inner_step(latents, target, timesteps, patch_weight, head_weight, modulation, time_weight):
    fsdp = lax.axis_size("fsdp")
    here = timesteps.shape[0]
    samples = here * fsdp
    width = patch_weight.shape[2]
    full = width * fsdp
    tok_count = latents.shape[0] * fsdp * 1.0
    f32 = jnp.float32

    sines = sinusoid(lax.all_gather(timesteps, "fsdp", tiled=True)).astype(jnp.bfloat16)
    wp = patch_weight[0].astype(jnp.bfloat16).astype(f32)
    wh = head_weight[0].astype(jnp.bfloat16).astype(f32)
    wm = modulation[0].astype(jnp.bfloat16).astype(f32)
    pre_act = jnp.dot(sines, time_weight[0].astype(jnp.bfloat16), preferred_element_type=f32)
    embed = jax.nn.silu(pre_act)
    gain = 1.0 + wm[1] + embed
    shift = wm[0] + embed

    mean_here = jnp.mean(wp, axis=1)
    wp_here = wp - mean_here[:, None]
    gained = wh[None] * gain[:, None, :]
    gram = fdot("if,kf->ik", wp_here, wp_here)
    mix = fdot("sjf,if->sij", gained, wp_here)
    gained_sum = jnp.sum(gained, axis=2)
    offset = fdot("sf,jf->sj", shift, wh)

    def split(a):
        return a.reshape(fsdp, -1, PATCH_DIM)

    def copies(a):
        return jnp.broadcast_to(a.reshape(1, -1, PATCH_DIM), (fsdp, a.size // PATCH_DIM, PATCH_DIM))

    sent = jnp.concatenate(
        [split(mix), split(gained_sum), split(offset), copies(gram), copies(mean_here)], axis=1
    )
    got = lax.all_to_all(sent, "fsdp", 0, 0)
    a, b = here * PATCH_DIM, here * PATCH_DIM + here
    mean_of = got[:, -1]
    mean = jnp.mean(mean_of, axis=0)
    off_mean = mean_of - mean
    gained_sum_of = got[:, a:b]
    mix = jnp.sum(got[:, :a], axis=0).reshape(here, PATCH_DIM, PATCH_DIM) + jnp.sum(
        off_mean[:, None, :, None] * gained_sum_of[:, :, None, :], axis=0
    )
    gained_mean = jnp.sum(gained_sum_of, axis=0) / full
    offset = jnp.sum(got[:, b : b + here], axis=0)
    gram = jnp.sum(got[:, b + here : -1], axis=0) + width * jnp.sum(
        off_mean[:, :, None] * off_mean[:, None, :], axis=0
    )
    gram = gram / full

    lat = latents.astype(f32)
    var = jnp.sum(fdot("ti,ik->tk", lat, gram) * lat, axis=1, keepdims=True)
    inv_std = lax.rsqrt(jnp.maximum(var, 0.0) + epsilon)
    lat = (lat * inv_std).reshape(here, SAMPLE_TOKENS, PATCH_DIM)
    centred = fdot("sti,sij->stj", lat, mix)
    wanted = target.reshape(here, SAMPLE_TOKENS, PATCH_DIM).astype(f32)
    output = centred + offset[:, None, :]
    grad_out = (2.0 * (output - wanted) / tok_count).astype(jnp.bfloat16).astype(f32)
    first = jnp.sum(grad_out * gained_mean[:, None, :], axis=2, keepdims=True)
    second = jnp.sum(grad_out * centred, axis=2, keepdims=True) / full
    cross = fdot("sti,stj->sij", lat, grad_out)
    square = fdot("sti,stk->ik", lat * second, lat)
    lean = jnp.sum(lat * first, axis=(0, 1))
    out_sum = jnp.sum(grad_out, axis=1)

    sent = jnp.concatenate(
        [cross.reshape(-1, PATCH_DIM), out_sum, square, lean[None]], axis=0
    )
    got = lax.all_gather(sent, "fsdp")
    cross = got[:, :a].reshape(samples, PATCH_DIM, PATCH_DIM)
    out_sum = got[:, a:b].reshape(samples, PATCH_DIM)
    square = jnp.sum(got[:, b:-1], axis=0)
    lean = jnp.sum(got[:, -1], axis=0)

    centre = wp - mean[:, None]
    turned = fdot("sij,if->sjf", cross, centre)
    grad_head = jnp.sum(turned * gain[:, None, :], axis=0) + fdot("sj,sf->jf", out_sum, shift)
    grad_scale = jnp.sum(turned * wh[None], axis=1)
    grad_shift = fdot("sj,jf->sf", out_sum, wh)
    grad_patch = (
        fdot("sij,sjf->if", cross, gained)
        - lean[:, None]
        - fdot("ik,kf->if", square, centre)
    )
    grad_mod = jnp.stack([jnp.sum(grad_shift, axis=0), jnp.sum(grad_scale, axis=0)])
    grad_pre = ((grad_shift + grad_scale) * silu_slope(pre_act)).astype(jnp.bfloat16)
    grad_time = lax.dot_general(
        sines, grad_pre, (((0,), (0,)), ((), ())), preferred_element_type=f32
    )
    return (
        patch_weight - inner_rate * grad_patch[None],
        head_weight - inner_rate * grad_head[None],
        modulation - inner_rate * grad_mod[None],
        time_weight - inner_rate * grad_time[None],
    )


def per_device(
    latents,
    target,
    timesteps,
    patch_weight,
    head_weight,
    modulation,
    time_weight,
    anchor,
    momentum,
    frag_start,
    frag_current,
):
    inner = inner_step(
        latents, target, timesteps, patch_weight, head_weight, modulation, time_weight
    )
    if lax.axis_size("replica") == 8 and anchor.shape[1] % 128 == 0:
        fragment = fragment_by_kernel
    else:
        fragment = fragment_by_collectives
    return inner + tuple(fragment(anchor, momentum, frag_start, frag_current[0]))


def solution(mesh):
    in_specs = (
        P(("replica", "fsdp"), None),
        P(("replica", "fsdp"), None),
        P(("replica", "fsdp")),
        P("replica", None, "fsdp"),
        P("replica", None, "fsdp"),
        P("replica", None, "fsdp"),
        P("replica", None, "fsdp"),
        P("fsdp", "replica"),
        P("fsdp", "replica"),
        P("fsdp", None),
        P("replica", "fsdp", None),
    )
    out_specs = (
        P("replica", None, "fsdp"),
        P("replica", None, "fsdp"),
        P("replica", None, "fsdp"),
        P("replica", None, "fsdp"),
        P("fsdp", "replica"),
        P("fsdp", "replica"),
        P("fsdp", None),
    )
    return jax.shard_map(
        per_device, mesh=mesh, in_specs=in_specs, out_specs=out_specs, check_vma=False
    )
```

time: 481 us -> 201 us (0.42)
  waiting for transfers between devices: 183 us -> 0.01 us
  Pallas kernels: 0 us -> 120 us
  other arithmetic: 112 us -> 6.08 us
  matrix products: 72.3 us -> 28.2 us
  local copies, waits for them, and re-layouts: 47.4 us -> 16 us
  blocking collectives: 48.8 us -> 25.1 us
  between operations: 15.7 us -> 1.68 us
    pallas_call x0 -> x1, Pallas kernels: none -> 120 us  [fragment_by_kernel(): pl.pallas_call(lambda *refs: fragment_kernel(blocks, cols, *refs), out_sh...]
    reduce_scatter x3 -> x0, waiting for transfers between devices: 95.8 us -> none  [the longest x1 52 us: per_device(): lax.psum_scatter(grad_time_full.astype(jnp.bfloat16), 'fsdp', scatter_dim...]
    all_gather x2 -> x0, waiting for transfers between devices: 73.3 us -> none  [the longest x1 73.2 us: per_device(): lax.all_gather(new_anchor.astype(jnp.bfloat16), 'replica', axis=1, tiled=...]
    convert_element_type x14 -> x2, other arithmetic: 66.8 us -> 0.74 us  [the longest x1 0.7 us: inner_step(): wm = modulation[0].astype(jnp.bfloat16).astype(f32)]
    dot_general x22 -> x14, matrix products: 72.3 us -> 28.2 us  [the longest x12 25.2 us: fdot(): jnp.einsum(spec, a, b, precision=EXACT, preferred_element_type=jnp.float32)]
    all_gather x3 -> x1, blocking collectives: 48.8 us -> 15.3 us  [inner_step(): got = lax.all_gather(sent, 'fsdp')]
    unnamed x22 -> x37, local copies, waits for them, and re-layouts: 35.9 us -> 12.4 us
    abs x1 -> x0, other arithmetic: 19.1 us -> none  [quantize(): seven_abs = 7.0 * jnp.abs(blocks)]
  transfers between devices with their start and end apart: 7 -> 1, of which waited for: 5 -> 0; matrix products, arithmetic and copies ran while one was open for 45% -> 0% of each run, Pallas kernels for 0% -> 60%
where the time goes in v1:
time: 201 us
  Pallas kernels  120 us (60%)
  matrix products  28.2 us (14%)
  blocking collectives  25.1 us (12%)
  local copies, waits for them, and re-layouts  16 us (8%)
  other arithmetic  6.08 us (3%)
  starting transfers between devices  3.64 us (2%)
    pallas_call x1, Pallas kernels, fragment_by_kernel(): pl.pallas_call(lambda *refs: fragment_kernel(blocks, cols, *refs), out_sh...  120 us
    dot_general x12, matrix products, fdot(): jnp.einsum(spec, a, b, precision=EXACT, preferred_element_type=jnp.float32)  25.2 us
    all_gather x1, blocking collectives, inner_step(): got = lax.all_gather(sent, 'fsdp')  15.3 us
    unnamed x37, local copies, waits for them, and re-layouts  12.4 us
    unnamed x1, blocking collectives  9.89 us
  transfers between devices with their start and end apart: 1, of which 0 were waited for; matrix products, arithmetic and copies ran while one was open for 0% of the time, Pallas kernels for 60%

profile of v1, /device:TPU:0, one launch (start us, length us, event | category | flops | bytes accessed | tf_op | source)
XLA Modules:
  0.0 200.9 jit_solution(2006003776131838344)
XLA Ops:
  0.6 0.0 copy-start.3
  0.6 0.0 copy-start.7
  0.7 1.3 dynamic-slice
  2.6 0.9 dynamic-update-slice
  3.5 9.9 %all-reduce = s32[16]{0:T(128)S(1)} all-reduce(s32[16]{0:T(128)S(1)} %dynamic-update-slice), channel_id=1, replica_groups=mesh['replica'=8,'fsdp'=4] {'fsdp'}, use_global_device_ids=true, to_apply=%add | all-reduce | flops 16 | bytes 128
  13.4 0.7 convert_convert_fusion
  14.1 1.1 convert_reduce_fusion.1
  15.2 1.0 bitcast_convert_fusion
  16.2 0.1 fusion.68
  16.4 0.5 fusion.45
  16.9 1.5 broadcast_add_fusion
  18.4 0.5 multiply_reduce_fusion
  18.9 7.8 %fusion.2 = f32[64,16,64]{2,0,1:T(8,128)S(1)} fusion(f32[16,1280]{1,0:T(8,128)S(1)} %get-tuple-element.30, f32[64,1280]{1,0:T(8,128)S(1)} %bitcast_convert_fusion, bf16[1,64,1280]{2,1,0:T(8,128)(2,1)S(1)} %get-tuple-element.27, f32[64]{0:T(128)S(1)} %broadcast_multiply_fusion.2), kind=kOutput, calls=%fused_computation.3 | convolution fusion | flops 1008107520 | bytes 835840 | tf_op jit(solution)/shard_map/sjf,if->sij/dot_general | solution.py:38
  26.7 0.0 copy-done.3
  26.7 0.8 fusion.51
  27.5 0.1 copy.100
  27.7 0.2 copy.99
  27.9 0.1 broadcast_in_dim.7
  27.9 0.9 concatenate.18
  28.9 3.6 %all-to-all-start = ((f32[4,329,64]{1,2,0:T(8,128)}), f32[4,329,64]{1,2,0:T(8,128)S(1)}, u32[]{:S(2)}, u32[]{:S(2)}) async-start(f32[4,329,64]{1,2,0:T(8,128)} %concatenate.18), calls=%async_computation | async-start | bytes 786432 | tf_op jit(solution)/shard_map/all_to_all | solution.py:380
  32.6 0.0 copy-start.5
  32.6 120.1 %fragment_sync.1 = (f32[1280,640]{1,0:T(8,128)}, f32[1280,640]{1,0:T(8,128)}, bf16[1280,5120]{1,0:T(8,128)(2,1)}) custom-call(bf16[1280,5120]{1,0:T(8,128)(2,1)} %refs_0_.1, bf16[1280,5120]{1,0:T(8,128)(2,1)} %bitcast.103, f32[1280,640]{1,0:T(8,128)} %refs_2_.1, f32[1280,640]{1,0:T(8,128)} %refs_3_.1), custom_call_target="tpu_custom_call" | custom-call | flops 131072000 | bytes 52428800 | tf_op jit(solution)/shard_map/fragment_sync/pallas_call | solution.py:290
  152.7 0.0 all-to-all-done
  152.7 0.2 slice_reduce_fusion.6
  153.0 0.2 subtract_reduce_fusion
  153.1 0.1 multiply_reduce_fusion.6
  153.3 0.1 copy.102
  153.3 0.1 slice_reduce_fusion.4
  153.5 0.4 fusion.23
  153.9 0.1 slice_reduce_fusion.8
  154.0 0.1 copy.112
  154.1 0.1 copy.109
  154.1 0.1 copy.105
  154.3 0.1 copy.124
  154.4 0.1 multiply_reduce_fusion.5
  154.5 0.8 convert_reduce_fusion
  155.4 0.4 fusion.35
  155.8 0.1 copy.113
  155.9 0.2 multiply_reduce_fusion.4
  156.1 0.6 fusion.24
  156.7 0.1 copy.114
  156.8 0.1 copy.115
  156.9 0.1 maximum_bitcast_fusion
  157.0 15.3 %all-gather.1 = f32[4,325,64]{1,2,0:T(8,128)S(1)} all-gather(f32[1,325,64]{1,2,0:T(8,128)S(1)} %maximum_bitcast_fusion), channel_id=2, replica_groups=mesh['replica'=8,'fsdp'=4] {'fsdp'}, dimensions={0}, use_global_device_ids=true | all-gather | bytes 416000 | tf_op jit(solution)/shard_map/all_gather | solution.py:414
  172.2 0.7 slice_reduce_fusion.2
  172.9 0.1 slice_reduce_fusion.1
  173.1 0.0 copy-start.4
  173.1 0.0 slice-start
  173.1 0.1 copy.118
  173.2 0.8 fusion.79
  174.0 0.6 stack.9
  174.6 1.0 copy.116
  175.7 6.2 %multiply_reduce_fusion.2 = (f32[16,1280]{1,0:T(8,128)S(1)}, f32[1280]{0:T(1024)S(1)}, f32[64,1280]{1,0:T(8,128)S(1)}) fusion(f32[64,1280]{1,0:T(8,128)S(1)} %bitcast_convert_fusion, f32[16,1280]{1,0:T(8,128)S(1)} %get-tuple-element.30, f32[16,64,64]{2,1,0:T(8,128)} %bitcast.109, bf16[1,64,1280]{2,1,0:T(8,128)(2,1)S(1)} %get-tuple-element.27, ...), kind=kOutput, calls=%fused_computation.6 | convolution fusion | flops 1013246720 | bytes 1250560 | tf_op jit(solution)/shard_map/sij,if->sjf/dot_general | solution.py:38
  181.9 4.4 %fusion.19 = f32[64,1280]{1,0:T(8,128)S(1)} fusion(f32[16,64,64]{2,1,0:T(8,128)} %bitcast.110, f32[16,1280]{1,0:T(8,128)S(1)} %get-tuple-element.30, f32[64,1280]{1,0:T(8,128)S(1)} %bitcast_convert_fusion, f32[64]{0:T(128)} %slice_reduce_fusion.2), kind=kOutput, calls=%fused_computation.24 | convolution fusion | flops 1008025600 | bytes 999680 | tf_op jit(solution)/shard_map/sij,sjf->if/dot_general | solution.py:38
  186.3 1.2 fusion.15
  187.5 1.2 fusion.13
  188.7 0.0 copy-done.8
  188.8 0.6 fusion.67
  189.4 0.0 copy-done.6
  189.4 1.4 fusion.5
  190.8 1.7 copy.145
  192.5 1.7 copy.146
  194.2 1.7 slice-done.3
  195.9 4.9 %copy.147 = bf16[1280,5120]{1,0:T(8,128)(2,1)} copy(bf16[1280,5120]{1,0:T(8,128)(2,1)S(1)} %bitcast.102) | data formatting | bytes 26214400
  (40 shorter events, 0.3 us)
Async XLA Ops:
  0.6 26.1 %copy-start.3 = (f32[1,64,1280]{2,1,0:T(8,128)S(1)}, f32[1,64,1280]{2,1,0:T(8,128)}, u32[]{:S(2)}) copy-start(f32[1,64,1280]{2,1,0:T(8,128)} %param.15) | copy-start | bytes 983044
  0.6 31.9 %copy-start.7 = (bf16[2048,64]{0,1:T(8,128)(2,1)S(1)}, bf16[2048,64]{0,1:T(8,128)(2,1)}, u32[]{:S(2)}) copy-start(bf16[2048,64]{0,1:T(8,128)(2,1)} %param.12) | copy-start | bytes 786436
  28.9 123.8 %all-to-all-start = ((f32[4,329,64]{1,2,0:T(8,128)}), f32[4,329,64]{1,2,0:T(8,128)S(1)}, u32[]{:S(2)}, u32[]{:S(2)}) async-start(f32[4,329,64]{1,2,0:T(8,128)} %concatenate.18), calls=%async_computation | async-start | bytes 786432 | tf_op jit(solution)/shard_map/all_to_all | solution.py:380
  32.6 120.9 %copy-start.5 = (bf16[2048,64]{0,1:T(8,128)(2,1)S(1)}, bf16[2048,64]{0,1:T(8,128)(2,1)}, u32[]{:S(2)}) copy-start(bf16[2048,64]{0,1:T(8,128)(2,1)} %param.11) | copy-start | bytes 786436
  173.1 14.5 %copy-start.4 = (f32[1,64,1280]{2,1,0:T(8,128)S(1)}, f32[1,64,1280]{2,1,0:T(8,128)}, u32[]{:S(2)}) copy-start(f32[1,64,1280]{2,1,0:T(8,128)} %param.14) | copy-start | bytes 983044
  173.1 21.2 %slice-start = ((s8[13107200]{0:T(1024)(128)(4,1)}), s8[524288]{0:T(1024)(128)(4,1)S(1)}, s32[]{:S(2)}) async-start(s8[13107200]{0:T(1024)(128)(4,1)} %bitcast.101), calls=%async_computation.1 | async-start | bytes 1048576
  174.6 14.1 %copy-start.8 = (f32[1,2,1280]{2,1,0:T(2,128)S(1)}, f32[1,2,1280]{2,1,0:T(2,128)}, u32[]{:S(2)}) copy-start(f32[1,2,1280]{2,1,0:T(2,128)} %param.16) | copy-start | bytes 30724
  174.6 14.7 %copy-start = (f32[1,256,1280]{2,1,0:T(8,128)S(1)}, f32[1,256,1280]{2,1,0:T(8,128)}, u32[]{:S(2)}) copy-start(f32[1,256,1280]{2,1,0:T(8,128)} %param.17) | copy-start | bytes 3932164
  175.6 13.1 %copy-start.9 = (f32[1,1,1280]{2,1,0:T(1,128)S(1)}, f32[1,1,1280]{2,1,0:T(1,128)}, u32[]{:S(2)}) copy-start(f32[1,1,1280]{2,1,0:T(1,128)} %stack.9) | copy-start | bytes 15364
  175.6 13.7 %copy-start.6 = (f32[16,1280]{1,0:T(8,128)S(1)}, f32[16,1280]{1,0:T(8,128)}, u32[]{:S(2)}) copy-start(f32[16,1280]{1,0:T(8,128)} %get-tuple-element.35) | copy-start | bytes 245764
  175.6 15.2 %copy-start.2 = (f32[1280,640]{1,0:T(8,128)S(1)}, f32[1280,640]{1,0:T(8,128)}, u32[]{:S(2)}) copy-start(f32[1280,640]{1,0:T(8,128)} %get-tuple-element.47) | copy-start | bytes 9830404
  175.6 18.6 %slice-start.1 = ((s8[13107200]{0:T(1024)(128)(4,1)}), s8[4194304]{0:T(1024)(128)(4,1)S(1)}, s32[]{:S(2)}) async-start(s8[13107200]{0:T(1024)(128)(4,1)} %bitcast.101), calls=%async_computation.2 | async-start | bytes 8388608
  187.5 5.0 %copy-start.1 = (f32[1280,640]{1,0:T(8,128)S(1)}, f32[1280,640]{1,0:T(8,128)}, u32[]{:S(2)}) copy-start(f32[1280,640]{1,0:T(8,128)} %get-tuple-element.48) | copy-start | bytes 9830404
  189.4 4.9 %slice-start.2 = ((s8[13107200]{0:T(1024)(128)(4,1)}), s8[4194304]{0:T(1024)(128)(4,1)S(1)}, s32[]{:S(2)}) async-start(s8[13107200]{0:T(1024)(128)(4,1)} %bitcast.101), calls=%async_computation.3 | async-start | bytes 8388608
  190.8 5.1 %slice-start.3 = ((s8[13107200]{0:T(1024)(128)(4,1)}), s8[4194304]{0:T(1024)(128)(4,1)S(1)}, s32[]{:S(2)}) async-start(s8[13107200]{0:T(1024)(128)(4,1)} %bitcast.101), calls=%async_computation.4 | async-start | bytes 8388608

commit v2 on v1

--- a/solution.py
+++ b/solution.py
@@ -46,13 +46,26 @@
     return index + bit - 2 * bit * lax.rem(index // bit, 2)
 
 
-def fragment_kernel(
+def window_kernel(
     blocks,
     cols,
+    peers,
+    here,
     start_hbm,
     cur_hbm,
     anchor_hbm,
     mom_hbm,
+    lat_in,
+    target_in,
+    sines_in,
+    patch_in,
+    head_in,
+    mod_in,
+    time_in,
+    patch_out,
+    head_out,
+    mod_out,
+    time_out,
     anchor_out,
     mom_out,
     params_out,
@@ -73,7 +86,28 @@
     g_send,
     g_recv,
     own_sem,
+    sines_all,
+    pre,
+    gain,
+    shift,
+    out1,
+    in1,
+    out2,
+    in2,
+    total1,
+    extra1,
+    wide,
+    scale_rows,
+    sum_rows,
+    z_send,
+    z_recv,
 ):
+    f32, bf16 = jnp.float32, jnp.bfloat16
+    z = lax.axis_index("fsdp")
+    width = patch_in.shape[1]
+    full = width * peers
+    group = here * PATCH_DIM
+    tok_count = here * SAMPLE_TOKENS * peers * 1.0
     me = lax.axis_index("replica")
     core = lax.rem(me, 2)
     rows = QBLOCK
@@ -177,7 +211,192 @@
         pl.semaphore_signal(
             barrier, inc=1, device_id={"replica": flip(me, bit)}, device_id_type=MESH
         )
-    pl.semaphore_wait(barrier, 3)
+    for k in range(1, peers):
+        pl.semaphore_signal(
+            barrier, inc=1, device_id={"fsdp": lax.rem(z + k, peers)}, device_id_type=MESH
+        )
+    pl.semaphore_wait(barrier, 3 + peers - 1)
+
+
+    def zsend(src, dst, what, k):
+        return pltpu.make_async_remote_copy(
+            src_ref=src,
+            dst_ref=dst,
+            send_sem=z_send.at[what, k - 1],
+            recv_sem=z_recv.at[what, k - 1],
+            device_id={"fsdp": lax.rem(z + k, peers)},
+            device_id_type=MESH,
+        )
+
+    def sines_copy(k):
+        return zsend(sines_in, sines_all.at[z], 0, k)
+
+    def first_copy(k):
+        return zsend(out1.at[k - 1], in1.at[z], 1, k)
+
+    def second_copy(k):
+        return zsend(out2, in2.at[z], 2, k)
+
+    def halves(values):
+        high = values.astype(bf16)
+        return high, (values - high.astype(f32)).astype(bf16)
+
+    def dot(a, b, dims):
+        return lax.dot_general(a, b, (dims, ((), ())), preferred_element_type=f32)
+
+    def dot2(a, b, dims):
+        high, low = halves(b)
+        return dot(a, high, dims) + dot(a, low, dims)
+
+    def dot3(a, b, dims):
+        a_high, a_low = halves(a)
+        b_high, b_low = halves(b)
+        return dot(a_high, b_high, dims) + dot(a_high, b_low, dims) + dot(a_low, b_high, dims)
+
+    nt, nn, tn = ((1,), (1,)), ((1,), (0,)), ((0,), (0,))
+
+    sines_all[z] = sines_in[...]
+    for k in range(1, peers):
+        sines_copy(k).start()
+
+    def rounded(ref):
+        return ref[...].astype(bf16).astype(f32)
+
+    def inner_open():
+        for k in range(1, peers):
+            sines_copy(k).wait()
+        sines = sines_all[...].reshape(peers * 8, FREQ_DIM).astype(bf16)
+        pre_act = dot(sines, time_in[...].astype(bf16), nn)
+        pre[...] = pre_act
+        embed = pre_act * jax.nn.sigmoid(pre_act)
+        mod = rounded(mod_in)
+        gain[...] = 1.0 + mod[1:2] + embed
+        shift[...] = mod[0:1] + embed
+
+    def inner_first(k):
+        to = lax.rem(z + k, peers)
+        rows8 = pl.ds(pl.multiple_of(to * 8, 8), 8)
+        raw = patch_in[...].astype(bf16)
+        wp = raw.astype(f32)
+        wp = wp - jnp.sum(wp, axis=1, keepdims=True) / width
+        wh = rounded(head_in)
+        gains = gain[rows8, :]
+        parts = [wh * gains[q : q + 1] for q in range(here)]
+        gained = jnp.concatenate(parts, axis=0)
+        mix = dot3(gained, wp, nt)
+        sums = jnp.sum(gained, axis=1, keepdims=True)
+        shift_high, shift_low = halves(shift[rows8, :])
+        head_bf = wh.astype(bf16)
+        offset = dot(shift_high, head_bf, nt) + dot(shift_low, head_bf, nt)
+        mean_rows = dot(jnp.ones((8, width), bf16), raw, nt) / width
+
+        def put(ref):
+            ref[pl.ds(0, group), 0:64] = mix
+            ref[pl.ds(0, group), 64:128] = jnp.broadcast_to(sums, (group, 64))
+            ref[pl.ds(group, 64), 0:64] = dot3(wp, wp, nt)
+            ref[pl.ds(group, 64), 64:128] = jnp.zeros((64, 64), f32)
+            ref[pl.ds(group + 64, 8), 0:64] = offset
+            ref[pl.ds(group + 64, 8), 64:128] = jnp.zeros((8, 64), f32)
+            ref[pl.ds(group + 72, 8), 0:64] = mean_rows
+            ref[pl.ds(group + 72, 8), 64:128] = jnp.zeros((8, 64), f32)
+
+        if k == 0:
+            put(in1.at[z])
+        else:
+            put(out1.at[k - 1])
+            first_copy(k).start()
+
+    def inner_gather():
+        for k in range(1, peers):
+            first_copy(k).wait()
+        means = [in1[d, pl.ds(group + 72, 8), 0:64] for d in range(peers)]
+        mean = sum(means[1:], means[0]) / peers
+        offs = [m - mean for m in means]
+        mix = jnp.zeros((group, 64), f32)
+        sums = jnp.zeros((group, 64), f32)
+        gram = jnp.zeros((64, 64), f32)
+        offset = jnp.zeros((8, 64), f32)
+        for d in range(peers):
+            wide_sum = in1[d, pl.ds(0, group), 64:128]
+            mix = mix + in1[d, pl.ds(0, group), 0:64] + wide_sum * offs[d][0:1]
+            sums = sums + wide_sum
+            gram = gram + in1[d, pl.ds(group, 64), 0:64]
+            gram = gram + (width / 8.0) * dot3(offs[d], offs[d], tn)
+            offset = offset + in1[d, pl.ds(group + 64, 8), 0:64]
+        total1[pl.ds(0, group), 0:64] = mix
+        total1[pl.ds(0, group), 64:128] = sums / full
+        total1[pl.ds(group, 64), 0:64] = gram / full
+        total1[pl.ds(group, 64), 64:128] = dot2(jnp.ones((64, 8), bf16), mean, nn).T / 8.0
+        extra1[...] = offset
+        out2[...] = jnp.zeros_like(out2)
+
+    def inner_sample(q):
+        span = pl.ds(q * SAMPLE_TOKENS, SAMPLE_TOKENS)
+        at = pl.ds(q * PATCH_DIM, PATCH_DIM)
+        lat_bf = lat_in[span, :]
+        lat = lat_bf.astype(f32)
+        gram = total1[pl.ds(group, 64), 0:64]
+        var = jnp.sum(dot2(lat_bf, gram, nn) * lat, axis=1, keepdims=True)
+        inv_std = lax.rsqrt(jnp.maximum(var, 0.0) + epsilon)
+        centred = dot2(lat_bf, total1[at, 0:64], nt) * inv_std
+        output = centred + extra1[q : q + 1, :]
+        grad_out = (2.0 * (output - target_in[span, :].astype(f32)) / tok_count).astype(bf16)
+        grad_f = grad_out.astype(f32)
+        first = dot2(grad_out, total1[at, 64:128], nn)
+        second = jnp.sum(grad_f * centred, axis=1, keepdims=True) / full
+        lat = lat * inv_std
+        wide[:, 0:64] = lat * second
+        wide[:, 64:128] = first
+        out2[at, 0:64] = dot2(grad_out, lat, tn)
+        out2[pl.ds(group, 64), :] += dot3(lat, wide[...], tn)
+        out2[pl.ds(group + 64 + q, 1), 0:64] = jnp.sum(grad_f, axis=0, keepdims=True)
+
+    def inner_second():
+        in2[z] = out2[...]
+        for k in range(1, peers):
+            second_copy(k).start()
+
+    def inner_close():
+        for k in range(1, peers):
+            second_copy(k).wait()
+        rest = in2[0, pl.ds(group, 64), :]
+        for d in range(1, peers):
+            rest = rest + in2[d, pl.ds(group, 64), :]
+        centre = rounded(patch_in) - total1[pl.ds(group, 64), 64:65]
+        patch_out[...] = patch_in[...] + inner_rate * (
+            rest[:, 64:65] + dot3(rest[:, 0:64], centre, nn)
+        )
+        for d in range(peers):
+            sum_rows[pl.ds(8 * d, 8), :] = in2[d, pl.ds(group + 64, 8), 0:64]
+        head_out[...] = head_in[...] - inner_rate * dot3(sum_rows[...], shift[...], tn)
+        scale_rows[...] = jnp.zeros_like(scale_rows)
+
+    def inner_source(d):
+        centre = rounded(patch_in) - total1[pl.ds(group, 64), 64:65]
+        wh = rounded(head_in)
+        cross = in2[d, pl.ds(0, group), 0:64]
+        turned = dot3(cross, centre, nn)
+        parts = []
+        head_sum = jnp.zeros_like(wh)
+        for q in range(here):
+            row = gain[8 * d + q : 8 * d + q + 1, :]
+            piece = turned[q * 64 : q * 64 + 64]
+            head_sum = head_sum + piece * row
+            scale_rows[8 * d + q : 8 * d + q + 1, :] = jnp.sum(piece * wh, axis=0, keepdims=True)
+            parts.append(wh * row)
+        head_out[...] -= inner_rate * head_sum
+        patch_out[...] -= inner_rate * dot3(cross, jnp.concatenate(parts, axis=0), tn)
+
+    def inner_end():
+        grad_scale = scale_rows[...]
+        high, low = halves(sum_rows[...])
+        head_bf = head_in[...].astype(bf16)
+        grad_shift = dot(high, head_bf, nn) + dot(low, head_bf, nn)
+        mod_out[0:1, :] = mod_in[0:1, :] - inner_rate * jnp.sum(grad_shift, axis=0, keepdims=True)
+        mod_out[1:2, :] = mod_in[1:2, :] - inner_rate * jnp.sum(grad_scale, axis=0, keepdims=True)
+        sines = sines_all[...].reshape(peers * 8, FREQ_DIM).astype(bf16)
+        grad_pre = ((grad_shift + grad_scale) * silu_slope(pre[...])).astype(bf16)
+        time_out[...] = time_in[...] - inner_rate * dot(sines, grad_pre, tn)
 
     def quantize(i):
         slot = lax.rem(i, 2)
@@ -259,7 +478,23 @@
 
     stages = ((0, quantize), (1, fold1), (3, fold2), (5, update), (7, spread2), (9, spread1))
 
+    parts = [(2, inner_open)]
+    parts += [(3 + k, lambda k=k: inner_first(peers - 1 - k)) for k in range(peers)]
+    at = 5 + peers
+    parts += [(at, inner_gather)]
+    parts += [(at + q, lambda q=q: inner_sample(q)) for q in range(here)]
+    at += here
+    parts += [(at - 1, inner_second), (at + 1, inner_close)]
+    parts += [(at + 1 + d, lambda d=d: inner_source(d)) for d in range(peers)]
+    parts += [(at + 1 + peers, inner_end)]
+
     def step(i, carry):
+        for when, part in parts:
+
+            @pl.when(i == when)
+            def _(part=part):
+                part()
+
         for lag, stage in stages:
 
             @pl.when(jnp.logical_and(i >= lag, i < blocks + lag))
@@ -268,7 +503,7 @@
 
         return carry
 
-    lax.fori_loop(0, blocks + stages[-1][0], step, 0)
+    lax.fori_loop(0, max(blocks + stages[-1][0], parts[-1][0] + 1), step, 0)
 
     def finish(i, carry):
         span = pl.ds(pl.multiple_of(i * rows, rows), rows)
@@ -282,23 +517,44 @@
     lax.fori_loop(0, blocks, finish, 0)
 
 
-def fragment_by_kernel(anchor, momentum, frag_start, frag_current):
-    rows, width = frag_start.shape
+def window_by_kernel(
+    latents,
+    target,
+    timesteps,
+    patch_weight,
+    head_weight,
+    modulation,
+    time_weight,
+    anchor,
+    momentum,
+    frag_start,
+    frag_current,
+):
+    rows, span = frag_start.shape
     blocks, cols = rows // QBLOCK, anchor.shape[1]
+    peers, here = lax.axis_size("fsdp"), timesteps.shape[0]
+    width = patch_weight.shape[2]
+    group = here * PATCH_DIM
     bf16, f32 = jnp.bfloat16, jnp.float32
     dma = pltpu.SemaphoreType.DMA
-    return pl.pallas_call(
-        lambda *refs: fragment_kernel(blocks, cols, *refs),
-        out_shape=(
+    sines = lax.reduce_precision(sinusoid(timesteps), 8, 7)
+    sines = jnp.pad(sines, ((0, 8 - here), (0, 0)))
+    params = (patch_weight[0], head_weight[0], modulation[0], time_weight[0])
+    out = pl.pallas_call(
+        lambda *refs: window_kernel(blocks, cols, peers, here, *refs),
+        out_shape=tuple(jax.ShapeDtypeStruct(p.shape, f32) for p in params)
+        + (
             jax.ShapeDtypeStruct((rows, cols), f32),
             jax.ShapeDtypeStruct((rows, cols), f32),
-            jax.ShapeDtypeStruct((rows, width), bf16),
+            jax.ShapeDtypeStruct((rows, span), bf16),
         ),
-        in_specs=[pl.BlockSpec(memory_space=pl.ANY)] * 4,
-        out_specs=(pl.BlockSpec(memory_space=pl.ANY),) * 3,
+        in_specs=[pl.BlockSpec(memory_space=pl.ANY)] * 4
+        + [pl.BlockSpec(memory_space=pltpu.VMEM)] * 7,
+        out_specs=(pl.BlockSpec(memory_space=pltpu.VMEM),) * 4
+        + (pl.BlockSpec(memory_space=pl.ANY),) * 3,
         scratch_shapes=[
-            pltpu.VMEM((2, QBLOCK, width), bf16),
-            pltpu.VMEM((2, QBLOCK, width), bf16),
+            pltpu.VMEM((2, QBLOCK, span), bf16),
+            pltpu.VMEM((2, QBLOCK, span), bf16),
             pltpu.VMEM((blocks, 2, 4, QBLOCK, cols), bf16),
             pltpu.VMEM((blocks, 4, QBLOCK, cols), bf16),
             pltpu.VMEM((blocks, 2, QBLOCK, cols), bf16),
@@ -314,15 +570,31 @@
             dma((7, blocks)),
             dma((7, blocks)),
             dma((blocks,)),
+            pltpu.VMEM((peers, 8, FREQ_DIM), f32),
+            pltpu.VMEM((peers * 8, width), f32),
+            pltpu.VMEM((peers * 8, width), f32),
+            pltpu.VMEM((peers * 8, width), f32),
+            pltpu.VMEM((peers - 1, group + 80, 128), f32),
+            pltpu.VMEM((peers, group + 80, 128), f32),
+            pltpu.VMEM((group + 72, 128), f32),
+            pltpu.VMEM((peers, group + 72, 128), f32),
+            pltpu.VMEM((group + 64, 128), f32),
+            pltpu.VMEM((8, 64), f32),
+            pltpu.VMEM((SAMPLE_TOKENS, 128), f32),
+            pltpu.VMEM((peers * 8, width), f32),
+            pltpu.VMEM((peers * 8, 64), f32),
+            dma((3, peers - 1)),
+            dma((3, peers - 1)),
         ],
         compiler_params=pltpu.CompilerParams(
-            collective_id=0, has_side_effects=True, vmem_limit_bytes=56 * 1024 * 1024
+            collective_id=0, has_side_effects=True, vmem_limit_bytes=60 * 1024 * 1024
         ),
         cost_estimate=pl.CostEstimate(
-            flops=20 * rows * width, bytes_accessed=8 * rows * width, transcendentals=0
+            flops=20 * rows * span, bytes_accessed=8 * rows * span, transcendentals=0
         ),
-        name="fragment_sync",
-    )(frag_start, frag_current, anchor, momentum)
+        name="window",
+    )(frag_start, frag_current, anchor, momentum, latents, target, sines, *params)
+    return tuple(o[None] for o in out[:4]) + tuple(out[4:])
 
 
 def fragment_by_collectives(anchor, momentum, frag_start, frag_current):
@@ -453,14 +725,12 @@
     frag_start,
     frag_current,
 ):
-    inner = inner_step(
-        latents, target, timesteps, patch_weight, head_weight, modulation, time_weight
-    )
-    if lax.axis_size("replica") == 8 and anchor.shape[1] % 128 == 0:
-        fragment = fragment_by_kernel
-    else:
-        fragment = fragment_by_collectives
-    return inner + tuple(fragment(anchor, momentum, frag_start, frag_current[0]))
+    inner = (latents, target, timesteps, patch_weight, head_weight, modulation, time_weight)
+    fragment = (anchor, momentum, frag_start, frag_current[0])
+    fits = anchor.shape[1] % 128 == 0 and timesteps.shape[0] <= 8
+    if lax.axis_size("replica") == 8 and 2 <= lax.axis_size("fsdp") <= 4 and fits:
+        return window_by_kernel(*inner, *fragment)
+    return inner_step(*inner) + tuple(fragment_by_collectives(*fragment))
 
 
 def solution(mesh):

time: 201 us -> 151 us (0.75)
  matrix products: 28.2 us -> 0 us
  blocking collectives: 25.1 us -> 0 us
  local copies, waits for them, and re-layouts: 16 us -> 23.3 us
  Pallas kernels: 120 us -> 126 us
  other arithmetic: 6.08 us -> 0.78 us
  starting transfers between devices: 3.64 us -> 0 us
    dot_general x14 -> x0, matrix products: 28.2 us -> none  [the longest x12 25.2 us: fdot(): jnp.einsum(spec, a, b, precision=EXACT, preferred_element_type=jnp.float32)]
    all_gather x1 -> x0, blocking collectives: 15.3 us -> none  [inner_step(): got = lax.all_gather(sent, 'fsdp')]
    unnamed x37 -> x13, local copies, waits for them, and re-layouts: 12.4 us -> 22.7 us
    unnamed x1 -> x0, blocking collectives: 9.89 us -> none
    pallas_call x1, Pallas kernels: 120 us -> 126 us  [window_by_kernel(): pl.pallas_call(lambda *refs: window_kernel(blocks, cols, peers, here, *re...]
    all_to_all x1 -> x0, starting transfers between devices: 3.64 us -> none  [inner_step(): got = lax.all_to_all(sent, 'fsdp', 0, 0)]
    reduce_sum x10 -> x0, other arithmetic: 3 us -> none  [the longest x1 1.09 us: inner_step(): mean_here = jnp.mean(wp, axis=1)]
  transfers between devices with their start and end apart: 1 -> 0, of which waited for: 0 -> 0; matrix products, arithmetic and copies ran while one was open for 0% -> 0% of each run, Pallas kernels for 60% -> 0%
where the time goes in v2:
time: 151 us
  Pallas kernels  126 us (83%)
  local copies, waits for them, and re-layouts  23.3 us (15%)
    pallas_call x1, Pallas kernels, window_by_kernel(): pl.pallas_call(lambda *refs: window_kernel(blocks, cols, peers, here, *re...  126 us
    unnamed x13, local copies, waits for them, and re-layouts  22.7 us

profile of v2, /device:TPU:0, one launch (start us, length us, event | category | flops | bytes accessed | tf_op | source)
XLA Modules:
  0.0 150.5 jit_solution(17407481398971730457)
XLA Ops:
  0.6 0.7 convert_element_type.5
  1.3 0.1 multiply_cosine_fusion
  1.4 0.6 pad.4.refs_6_
  2.0 2.0 %copy.18.refs_4_ = bf16[2048,64]{1,0:T(8,128)(2,1)} copy(bf16[2048,64]{0,1:T(8,128)(2,1)} %param.11) | data formatting | bytes 524288 | tf_op args[0]
  4.0 2.0 %copy.19.refs_5_ = bf16[2048,64]{1,0:T(8,128)(2,1)} copy(bf16[2048,64]{0,1:T(8,128)(2,1)} %param.12) | data formatting | bytes 524288 | tf_op args[1]
  5.9 125.8 %window.1 = (f32[64,1280]{1,0:T(8,128)}, f32[64,1280]{1,0:T(8,128)}, f32[2,1280]{1,0:T(2,128)}, f32[256,1280]{1,0:T(8,128)}, f32[1280,640]{1,0:T(8,128)}, /*inde...) custom-call(bf16[1280,5120]{1,0:T(8,128)(2,1)} %refs_0_.1, bf16[1280,5120]{1,0:T(8,128)(2,1)} %bitcast.9, f32[1280,640]{1,0:T(8,128)} %refs_2_.1, ...), custom_call_target="tpu_custom_call" | custom-call | flops 131072000 | bytes 52428800 | tf_op jit(solution)/shard_map/window/pallas_call | solution.py:543
  131.8 1.7 %copy.27 = f32[1,64,1280]{2,1,0:T(8,128)} copy(f32[1,64,1280]{2,1,0:T(8,128)} %bitcast.15) | data formatting | bytes 655360
  133.5 0.0 copy-start.1
  133.5 1.9 %copy.28 = f32[1,64,1280]{2,1,0:T(8,128)} copy(f32[1,64,1280]{2,1,0:T(8,128)} %bitcast.14) | data formatting | bytes 655360
  135.4 1.3 copy.29
  136.7 0.0 copy-start
  136.7 2.6 %copy.30 = f32[1,256,1280]{2,1,0:T(8,128)} copy(f32[1,256,1280]{2,1,0:T(8,128)} %bitcast.11) | data formatting | bytes 2621440
  139.3 4.6 %copy.31 = f32[1280,640]{1,0:T(8,128)} copy(f32[1280,640]{1,0:T(8,128)} %get-tuple-element.34) | data formatting | bytes 6553600
  143.9 0.0 copy-done.1
  143.9 1.7 %copy.32 = f32[1280,640]{1,0:T(8,128)} copy(f32[1280,640]{1,0:T(8,128)S(1)} %copy-done.1) | data formatting | bytes 6553600
  145.6 0.0 copy-done
  145.6 4.9 %copy.33 = bf16[1280,5120]{1,0:T(8,128)(2,1)} copy(bf16[1280,5120]{1,0:T(8,128)(2,1)S(1)} %copy-done) | data formatting | bytes 26214400
  (2 shorter events, 0.0 us)
Async XLA Ops:
  133.5 10.4 %copy-start.1 = (f32[1280,640]{1,0:T(8,128)S(1)}, f32[1280,640]{1,0:T(8,128)}, u32[]{:S(2)}) copy-start(f32[1280,640]{1,0:T(8,128)} %get-tuple-element.35) | copy-start | bytes 9830404
  136.7 8.9 %copy-start = (bf16[1280,5120]{1,0:T(8,128)(2,1)S(1)}, bf16[1280,5120]{1,0:T(8,128)(2,1)}, u32[]{:S(2)}) copy-start(bf16[1280,5120]{1,0:T(8,128)(2,1)} %get-tuple-element.36) | copy-start | bytes 39321604

commit v3 on v2

--- a/solution.py
+++ b/solution.py
@@ -96,7 +96,6 @@
     in2,
     total1,
     extra1,
-    wide,
     scale_rows,
     sum_rows,
     z_send,
@@ -137,7 +136,8 @@
     def pair_at(who, fixed, other, k):
         chip = who // 2
         f, o = fixed // 2, other // 2
-        return f * lax.rem(chip // f, 2) + o * k
+        mine = lax.rem(chip // o, 2)
+        return f * lax.rem(chip // f, 2) + o * (mine if k == 1 else 1 - mine)
 
     def step1(i):
         return send(
@@ -287,7 +287,7 @@
         sums = jnp.sum(gained, axis=1, keepdims=True)
         shift_high, shift_low = halves(shift[rows8, :])
         head_bf = wh.astype(bf16)
-        offset = dot(shift_high, head_bf, nt) + dot(shift_low, head_bf, nt)
+        offset = dot(head_bf, shift_high, nt) + dot(head_bf, shift_low, nt)
         mean_rows = dot(jnp.ones((8, width), bf16), raw, nt) / width
 
         def put(ref):
@@ -295,10 +295,9 @@
             ref[pl.ds(0, group), 64:128] = jnp.broadcast_to(sums, (group, 64))
             ref[pl.ds(group, 64), 0:64] = dot3(wp, wp, nt)
             ref[pl.ds(group, 64), 64:128] = jnp.zeros((64, 64), f32)
-            ref[pl.ds(group + 64, 8), 0:64] = offset
+            ref[pl.ds(group, 64), 64:72] = offset
+            ref[pl.ds(group + 64, 8), 0:64] = mean_rows
             ref[pl.ds(group + 64, 8), 64:128] = jnp.zeros((8, 64), f32)
-            ref[pl.ds(group + 72, 8), 0:64] = mean_rows
-            ref[pl.ds(group + 72, 8), 64:128] = jnp.zeros((8, 64), f32)
 
         if k == 0:
             put(in1.at[z])
@@ -309,47 +308,50 @@
     def inner_gather():
         for k in range(1, peers):
             first_copy(k).wait()
-        means = [in1[d, pl.ds(group + 72, 8), 0:64] for d in range(peers)]
+        means = [in1[d, pl.ds(group + 64, 8), 0:64] for d in range(peers)]
         mean = sum(means[1:], means[0]) / peers
         offs = [m - mean for m in means]
         mix = jnp.zeros((group, 64), f32)
         sums = jnp.zeros((group, 64), f32)
         gram = jnp.zeros((64, 64), f32)
-        offset = jnp.zeros((8, 64), f32)
+        offset = jnp.zeros((64, 8), f32)
         for d in range(peers):
             wide_sum = in1[d, pl.ds(0, group), 64:128]
             mix = mix + in1[d, pl.ds(0, group), 0:64] + wide_sum * offs[d][0:1]
             sums = sums + wide_sum
             gram = gram + in1[d, pl.ds(group, 64), 0:64]
             gram = gram + (width / 8.0) * dot3(offs[d], offs[d], tn)
-            offset = offset + in1[d, pl.ds(group + 64, 8), 0:64]
+            offset = offset + in1[d, pl.ds(group, 64), 64:72]
         total1[pl.ds(0, group), 0:64] = mix
         total1[pl.ds(0, group), 64:128] = sums / full
         total1[pl.ds(group, 64), 0:64] = gram / full
         total1[pl.ds(group, 64), 64:128] = dot2(jnp.ones((64, 8), bf16), mean, nn).T / 8.0
-        extra1[...] = offset
+        extra1[:, 0:8] = offset
         out2[...] = jnp.zeros_like(out2)
 
     def inner_sample(q):
         span = pl.ds(q * SAMPLE_TOKENS, SAMPLE_TOKENS)
         at = pl.ds(q * PATCH_DIM, PATCH_DIM)
-        lat_bf = lat_in[span, :]
+        lat_bf = lat_in[:, span]
         lat = lat_bf.astype(f32)
-        gram = total1[pl.ds(group, 64), 0:64]
-        var = jnp.sum(dot2(lat_bf, gram, nn) * lat, axis=1, keepdims=True)
+        gram_high, gram_low = halves(total1[pl.ds(group, 64), 0:64])
+        mix_high, mix_low = halves(total1[at, 0:64])
+        spread = dot(gram_high, lat_bf, nn) + dot(gram_low, lat_bf, nn)
+        var = jnp.sum(spread * lat, axis=0, keepdims=True)
         inv_std = lax.rsqrt(jnp.maximum(var, 0.0) + epsilon)
-        centred = dot2(lat_bf, total1[at, 0:64], nt) * inv_std
-        output = centred + extra1[q : q + 1, :]
-        grad_out = (2.0 * (output - target_in[span, :].astype(f32)) / tok_count).astype(bf16)
+        centred = (dot(mix_high, lat_bf, nn) + dot(mix_low, lat_bf, nn)) * inv_std
+        output = centred + extra1[:, q : q + 1]
+        grad_out = (2.0 * (output - target_in[:, span].astype(f32)) / tok_count).astype(bf16)
         grad_f = grad_out.astype(f32)
-        first = dot2(grad_out, total1[at, 64:128], nn)
-        second = jnp.sum(grad_f * centred, axis=1, keepdims=True) / full
+        first = jnp.sum(grad_f * total1[at, 64:65], axis=0, keepdims=True)
+        second = jnp.sum(grad_f * centred, axis=0, keepdims=True) / full
         lat = lat * inv_std
-        wide[:, 0:64] = lat * second
-        wide[:, 64:128] = first
-        out2[at, 0:64] = dot2(grad_out, lat, tn)
-        out2[pl.ds(group, 64), :] += dot3(lat, wide[...], tn)
-        out2[pl.ds(group + 64 + q, 1), 0:64] = jnp.sum(grad_f, axis=0, keepdims=True)
+        out2[at, 0:64] = dot2(grad_out, lat, nt)
+        out2[pl.ds(group, 64), 0:64] += dot3(lat, lat * second, nt)
+        lean = jnp.sum(lat * first, axis=1, keepdims=True)
+        out2[pl.ds(group, 64), 64:128] += jnp.broadcast_to(lean, (64, 64))
+        sums = dot(jnp.ones((8, SAMPLE_TOKENS), bf16), grad_out, nt)
+        out2[pl.ds(group + 64 + q, 1), 0:64] = sums[0:1]
 
     def inner_second():
         in2[z] = out2[...]
@@ -433,15 +435,15 @@
             copy.start()
 
     def fold2(i):
-        for copy in step2(i):
+        first, second = bits(i)
+        for k, copy in enumerate(step2(i)):
             copy.wait()
-        first, second = bits(i)
-        for k in range(2):
             at = pair_at(me, first, second, k)
             terms[i, core, at] = (
                 terms[i, core, at].astype(jnp.float32) + got2[i, k].astype(jnp.float32)
             ).astype(jnp.bfloat16)
-        step3(i).start()
+            if k == 0:
+                step3(i).start()
 
     def update(i):
         step3(i).wait()
@@ -461,22 +463,24 @@
         anchor_v[span, :] = new_anchor
         own[i] = new_anchor.astype(jnp.bfloat16)
         back3(i).start()
+        back2(i)[0].start()
+        back1(i)[0].start()
         keep(i).start()
         pltpu.make_async_copy(anchor_v.at[span, :], anchor_out.at[span, :], store_sem.at[0, i]).start()
         pltpu.make_async_copy(mom_v.at[span, :], mom_out.at[span, :], store_sem.at[1, i]).start()
 
     def spread2(i):
         back3(i).wait()
-        for copy in back2(i):
-            copy.start()
+        back2(i)[1].start()
+        back1(i)[1].start()
 
     def spread1(i):
-        for copy in back2(i):
+        for n, copy in enumerate(back2(i)):
             copy.wait()
-        for copy in back1(i):
-            copy.start()
-
-    stages = ((0, quantize), (1, fold1), (3, fold2), (5, update), (7, spread2), (9, spread1))
+            back1(i)[2 + n].start()
+
+    stages = ((9, spread1), (7, spread2), (5, update), (0, quantize), (1, fold1), (3, fold2))
+    last = max(lag for lag, _ in stages)
 
     parts = [(2, inner_open)]
     parts += [(3 + k, lambda k=k: inner_first(peers - 1 - k)) for k in range(peers)]
@@ -489,21 +493,21 @@
     parts += [(at + 1 + peers, inner_end)]
 
     def step(i, carry):
+        for lag, stage in stages:
+
+            @pl.when(jnp.logical_and(i >= lag, i < blocks + lag))
+            def _(stage=stage, lag=lag):
+                stage(i - lag)
+
         for when, part in parts:
 
             @pl.when(i == when)
             def _(part=part):
                 part()
 
-        for lag, stage in stages:
-
-            @pl.when(jnp.logical_and(i >= lag, i < blocks + lag))
-            def _(stage=stage, lag=lag):
-                stage(i - lag)
-
         return carry
 
-    lax.fori_loop(0, max(blocks + stages[-1][0], parts[-1][0] + 1), step, 0)
+    lax.fori_loop(0, max(blocks + last, parts[-1][0] + 1), step, 0)
 
     def finish(i, carry):
         span = pl.ds(pl.multiple_of(i * rows, rows), rows)
@@ -515,6 +519,47 @@
         return carry
 
     lax.fori_loop(0, blocks, finish, 0)
+
+
+def hand_on(arrays):
+    pieces = []
+    for n, a in enumerate(arrays):
+        rows = a.shape[0]
+        size = QBLOCK if rows % QBLOCK == 0 else rows
+        pieces += [(n, at, size) for at in range(0, rows, size)]
+
+    def kernel(*refs):
+        count = len(arrays)
+        ins, outs, held = refs[:count], refs[count : 2 * count], refs[2 * count : 3 * count]
+        load_sem, store_sem = refs[3 * count :]
+
+        def moves(k):
+            n, at, size = pieces[k]
+            rows = pl.ds(at, size)
+            return (
+                pltpu.make_async_copy(ins[n].at[rows], held[n].at[rows], load_sem.at[k]),
+                pltpu.make_async_copy(held[n].at[rows], outs[n].at[rows], store_sem.at[k]),
+            )
+
+        for k in range(len(pieces)):
+            moves(k)[0].start()
+        for k in range(len(pieces)):
+            moves(k)[0].wait()
+            moves(k)[1].start()
+        for k in range(len(pieces)):
+            moves(k)[1].wait()
+
+    dma = pltpu.SemaphoreType.DMA
+    return pl.pallas_call(
+        kernel,
+        out_shape=tuple(jax.ShapeDtypeStruct(a.shape, a.dtype) for a in arrays),
+        in_specs=[pl.BlockSpec(memory_space=pl.ANY)] * len(arrays),
+        out_specs=(pl.BlockSpec(memory_space=pl.ANY),) * len(arrays),
+        scratch_shapes=[pltpu.VMEM(a.shape, a.dtype) for a in arrays]
+        + [dma((len(pieces),)), dma((len(pieces),))],
+        compiler_params=pltpu.CompilerParams(vmem_limit_bytes=60 * 1024 * 1024),
+        name="hand_on",
+    )(*arrays)
 
 
 def window_by_kernel(
@@ -574,13 +619,12 @@
             pltpu.VMEM((peers * 8, width), f32),
             pltpu.VMEM((peers * 8, width), f32),
             pltpu.VMEM((peers * 8, width), f32),
-            pltpu.VMEM((peers - 1, group + 80, 128), f32),
-            pltpu.VMEM((peers, group + 80, 128), f32),
+            pltpu.VMEM((peers - 1, group + 72, 128), f32),
+            pltpu.VMEM((peers, group + 72, 128), f32),
             pltpu.VMEM((group + 72, 128), f32),
             pltpu.VMEM((peers, group + 72, 128), f32),
             pltpu.VMEM((group + 64, 128), f32),
-            pltpu.VMEM((8, 64), f32),
-            pltpu.VMEM((SAMPLE_TOKENS, 128), f32),
+            pltpu.VMEM((64, 128), f32),
             pltpu.VMEM((peers * 8, width), f32),
             pltpu.VMEM((peers * 8, 64), f32),
             dma((3, peers - 1)),
@@ -593,7 +637,8 @@
             flops=20 * rows * span, bytes_accessed=8 * rows * span, transcendentals=0
         ),
         name="window",
-    )(frag_start, frag_current, anchor, momentum, latents, target, sines, *params)
+    )(frag_start, frag_current, anchor, momentum, latents.T, target.T, sines, *params)
+    out = hand_on(out)
     return tuple(o[None] for o in out[:4]) + tuple(out[4:])
 
 

time: 151 us -> 143 us (0.947)
  local copies, waits for them, and re-layouts: 23.3 us -> 0.61 us
  Pallas kernels: 126 us -> 141 us
    unnamed x13 -> x0, local copies, waits for them, and re-layouts: 22.7 us -> none
    pallas_call x0 -> x1, Pallas kernels: none -> 15.5 us  [hand_on(): pl.pallas_call(kernel, out_shape=tuple((jax.ShapeDtypeStruct(a.shape, a.d...]
where the time goes in v3:
time: 143 us
  Pallas kernels  141 us (99%)
    pallas_call x1, Pallas kernels, window_by_kernel(): pl.pallas_call(lambda *refs: window_kernel(blocks, cols, peers, here, *re...  125 us
    pallas_call x1, Pallas kernels, hand_on(): pl.pallas_call(kernel, out_shape=tuple((jax.ShapeDtypeStruct(a.shape, a.d...  15.5 us

profile of v3, /device:TPU:0, one launch (start us, length us, event | category | flops | bytes accessed | tf_op | source)
XLA Modules:
  0.0 142.7 jit_solution(12914955653928246838)
XLA Ops:
  0.6 0.7 convert_element_type.5
  1.3 0.1 multiply_cosine_fusion
  1.4 0.6 pad.4.refs_6_
  2.0 125.2 %window.1 = (f32[64,1280]{1,0:T(8,128)}, f32[64,1280]{1,0:T(8,128)}, f32[2,1280]{1,0:T(2,128)}, f32[256,1280]{1,0:T(8,128)}, f32[1280,640]{1,0:T(8,128)}, /*inde...) custom-call(bf16[1280,5120]{1,0:T(8,128)(2,1)} %refs_0_.1, bf16[1280,5120]{1,0:T(8,128)(2,1)} %bitcast.11, f32[1280,640]{1,0:T(8,128)} %refs_2_.1, ...), custom_call_target="tpu_custom_call" | custom-call | flops 131072000 | bytes 52428800 | tf_op jit(solution)/shard_map/window/pallas_call | solution.py:588
  127.2 15.5 %hand_on.1 = (f32[64,1280]{1,0:T(8,128)}, f32[64,1280]{1,0:T(8,128)}, f32[2,1280]{1,0:T(2,128)}, f32[256,1280]{1,0:T(8,128)}, f32[1280,640]{1,0:T(8,128)}, /*ind...) custom-call(f32[64,1280]{1,0:T(8,128)} %get-tuple-element.21.refs_0_, f32[64,1280]{1,0:T(8,128)} %get-tuple-element.22.refs_1_, ...), custom_call_target="tpu_custom_call" | custom-call | tf_op jit(solution)/shard_map/hand_on/pallas_call | solution.py:553
  (2 shorter events, 0.0 us)

commit v4 on v3

--- a/solution.py
+++ b/solution.py
@@ -530,24 +530,17 @@
 
     def kernel(*refs):
         count = len(arrays)
-        ins, outs, held = refs[:count], refs[count : 2 * count], refs[2 * count : 3 * count]
-        load_sem, store_sem = refs[3 * count :]
-
-        def moves(k):
+        ins, outs, sem = refs[:count], refs[count : 2 * count], refs[2 * count]
+
+        def move(k):
             n, at, size = pieces[k]
             rows = pl.ds(at, size)
-            return (
-                pltpu.make_async_copy(ins[n].at[rows], held[n].at[rows], load_sem.at[k]),
-                pltpu.make_async_copy(held[n].at[rows], outs[n].at[rows], store_sem.at[k]),
-            )
+            return pltpu.make_async_copy(ins[n].at[rows], outs[n].at[rows], sem.at[k])
 
         for k in range(len(pieces)):
-            moves(k)[0].start()
+            move(k).start()
         for k in range(len(pieces)):
-            moves(k)[0].wait()
-            moves(k)[1].start()
-        for k in range(len(pieces)):
-            moves(k)[1].wait()
+            move(k).wait()
 
     dma = pltpu.SemaphoreType.DMA
     return pl.pallas_call(
@@ -555,8 +548,7 @@
         out_shape=tuple(jax.ShapeDtypeStruct(a.shape, a.dtype) for a in arrays),
         in_specs=[pl.BlockSpec(memory_space=pl.ANY)] * len(arrays),
         out_specs=(pl.BlockSpec(memory_space=pl.ANY),) * len(arrays),
-        scratch_shapes=[pltpu.VMEM(a.shape, a.dtype) for a in arrays]
-        + [dma((len(pieces),)), dma((len(pieces),))],
+        scratch_shapes=[dma((len(pieces),))],
         compiler_params=pltpu.CompilerParams(vmem_limit_bytes=60 * 1024 * 1024),
         name="hand_on",
     )(*arrays)

time: 143 us -> 784 us (5.48)
  Pallas kernels: 141 us -> 782 us
    pallas_call x1, Pallas kernels: 15.5 us -> 657 us  [hand_on(): pl.pallas_call(kernel, out_shape=tuple((jax.ShapeDtypeStruct(a.shape, a.d...]
where the time goes in v4:
time: 784 us
  Pallas kernels  782 us (100%)
    pallas_call x1, Pallas kernels, hand_on(): pl.pallas_call(kernel, out_shape=tuple((jax.ShapeDtypeStruct(a.shape, a.d...  657 us
    pallas_call x1, Pallas kernels, window_by_kernel(): pl.pallas_call(lambda *refs: window_kernel(blocks, cols, peers, here, *re...  125 us

profile of v4, /device:TPU:0, one launch (start us, length us, event | category | flops | bytes accessed | tf_op | source)
XLA Modules:
  0.0 784.1 jit_solution(17653056517490594736)
XLA Ops:
  0.6 0.7 convert_element_type.5
  1.3 0.1 multiply_cosine_fusion
  1.4 0.6 pad.4.refs_6_
  2.0 125.2 %window.1 = (f32[64,1280]{1,0:T(8,128)}, f32[64,1280]{1,0:T(8,128)}, f32[2,1280]{1,0:T(2,128)}, f32[256,1280]{1,0:T(8,128)}, f32[1280,640]{1,0:T(8,128)}, /*inde...) custom-call(bf16[1280,5120]{1,0:T(8,128)(2,1)} %refs_0_.1, bf16[1280,5120]{1,0:T(8,128)(2,1)} %bitcast.11, f32[1280,640]{1,0:T(8,128)} %refs_2_.1, ...), custom_call_target="tpu_custom_call" | custom-call | flops 131072000 | bytes 52428800 | tf_op jit(solution)/shard_map/window/pallas_call | solution.py:580
  127.2 656.9 %hand_on.1 = (f32[64,1280]{1,0:T(8,128)}, f32[64,1280]{1,0:T(8,128)}, f32[2,1280]{1,0:T(2,128)}, f32[256,1280]{1,0:T(8,128)}, f32[1280,640]{1,0:T(8,128)}, /*ind...) custom-call(f32[64,1280]{1,0:T(8,128)} %get-tuple-element.21.refs_0_, f32[64,1280]{1,0:T(8,128)} %get-tuple-element.22.refs_1_, ...), custom_call_target="tpu_custom_call" | custom-call | tf_op jit(solution)/shard_map/hand_on/pallas_call | solution.py:546
  (2 shorter events, 0.0 us)
